TPU v7x, 32 devices: a whole 2x2x4 slice. The times are simulated.
32 devices in a mesh: section: 2 (over x), grp: 16 (over z, y, core).
Axes of the slice: x: 2, y: 2, z: 4, core: 2. Of those that a mesh axis runs over, the one named last changes fastest.
Arguments:
- voltages: bfloat16 [1024, 524288], P('grp', 'section'), may hold values from -6 to 6
- filter_taps: float32 [8, 512], replicated, may hold values from -2 to 2
- beam_weights: bfloat16 [256, 2, 512, 1024], P('grp'), may hold values from -0.125 to 0.125
- antenna_of_row: int32 [1024], replicated, may hold values from 0 to 1023, each once
- beam_delay: int32 [512], P('grp'), may hold values from 0 to 127
Outputs:
- dedispersed: float32 [256, 2, 512, 1024], P(None, None, 'grp', 'section')
Inputs may be any that keep to these rules, and one draw needn't show every extreme that they name: A permutation: voltage row r holds physical antenna antenna_of_row[r].
All inputs are finite; a program needn't handle non-finite values.
Results may differ from a plain program's by a relative error of at most 0.0069.
Values may be sent and summed in bfloat16 or wider, within the bound.
No kernel may reach another device: no remote copies, remote signals or barrier semaphores. Data moves between devices by JAX's collectives and lax.ppermute only.
A program may use at most 320 MiB of HBM per device.

v0:
```python
import math

import jax
import jax.numpy as jnp
from jax import lax
from jax.sharding import PartitionSpec as P

DFT_LEN = 256


def shifted(value, axis, steps):
    count = lax.axis_size(axis)
    leading, last = (max(0, -steps), min(count, count - steps))
    return lax.ppermute(value, axis, [(source, source + steps) for source in range(leading, last)])


def dft_table(frame_length, group_count, split_ways):
    channels = frame_length // 2
    per_target = channels // (group_count * split_ways)
    column = jnp.arange(frame_length, dtype=jnp.int32)
    target = column // (2 * per_target)
    within = column % (2 * per_target)
    quadrature = within // per_target
    channel = (
        target % group_count * (per_target * split_ways)
        + target // group_count * per_target
        + within % per_target
    )
    sample = jnp.arange(frame_length, dtype=jnp.int32)[:, None]
    winding = sample * channel[None, :] % frame_length
    angles = 2.0 * math.pi / frame_length * winding.astype(jnp.float32)
    factor = channels ** (-0.5)
    dft_cols = jnp.where(
        quadrature[None, :] == 0, jnp.cos(angles) * factor, -jnp.sin(angles) * factor
    )
    return dft_cols.astype(jnp.bfloat16)


def block_tables(length):
    half_len = length // 2
    factor = length ** (-0.5)
    sample = jnp.arange(length, dtype=jnp.int32)
    angles = (
        2.0 * math.pi / length * (sample[:, None] * sample[None, :] % length).astype(jnp.float32)
    )
    cosine_table = (jnp.cos(angles) * factor).astype(jnp.bfloat16)
    sine_table = (jnp.sin(angles) * factor).astype(jnp.bfloat16)
    forward_real = jnp.concatenate([cosine_table, -sine_table], axis=1)
    forward_imag = jnp.concatenate([sine_table, cosine_table], axis=1)
    back_cos = cosine_table[:, half_len:]
    back_sin = sine_table[:, half_len:]
    inverse_real = jnp.concatenate([back_cos, back_sin], axis=1)
    inverse_imag = jnp.concatenate([-back_sin, back_cos], axis=1)
    return (forward_real, forward_imag, inverse_real, inverse_imag)


def chirp_factor(delays, channel_count, channels, length):
    frequency = jnp.arange(length, dtype=jnp.int32)
    signed = jnp.where(frequency < length // 2, frequency, frequency - length).astype(jnp.float32)
    channel = jnp.arange(channel_count, dtype=jnp.int32).astype(jnp.float32)
    strength = (1.0 + channel / channels) ** (-3.0)
    sweep = signed * signed / (length * length)
    phases = (math.pi * delays.astype(jnp.float32))[None, :, None] * strength[
        :, None, None
    ] * sweep[None, None, :] - 0.5 * math.pi * frequency.astype(jnp.float32)[None, None, :]
    return (jnp.cos(phases), jnp.sin(phases))


def dedisperse(series, leading, delays, tables, channels):
    forward_real, forward_imag, inverse_real, inverse_imag = tables
    length = forward_real.shape[0]
    advance = length // 2
    chan_count = series.shape[0]
    beam_count = series.shape[2]
    time_len = series.shape[3]
    block_count = time_len // advance
    joined = jnp.concatenate([leading, series], axis=3).reshape(
        chan_count, 2, beam_count, block_count + 1, advance
    )
    blocks = jnp.concatenate([joined[:, :, :, :-1, :], joined[:, :, :, 1:, :]], axis=4)
    spectrum = jnp.einsum(
        "cbml,lk->cbmk", blocks[:, 0], forward_real, preferred_element_type=jnp.float32
    ) + jnp.einsum("cbml,lk->cbmk", blocks[:, 1], forward_imag, preferred_element_type=jnp.float32)
    chirp_real, chirp_imag = chirp_factor(delays, chan_count, channels, length)
    chirp_real = chirp_real[:, :, None, :]
    chirp_imag = chirp_imag[:, :, None, :]
    spec_real = spectrum[..., :length]
    spec_imag = spectrum[..., length:]
    filtered_real = (spec_real * chirp_real - spec_imag * chirp_imag).astype(jnp.bfloat16)
    filtered_imag = (spec_real * chirp_imag + spec_imag * chirp_real).astype(jnp.bfloat16)
    result = jnp.einsum(
        "cbmk,kn->cbmn", filtered_real, inverse_real, preferred_element_type=jnp.float32
    ) + jnp.einsum("cbmk,kn->cbmn", filtered_imag, inverse_imag, preferred_element_type=jnp.float32)
    out_real = result[..., :advance].reshape(chan_count, beam_count, time_len)
    out_imag = result[..., advance:].reshape(chan_count, beam_count, time_len)
    return jnp.stack([out_real, out_imag], axis=1)


def local(voltages, filter_taps, beam_weights, antenna_of_row, beam_delay):
    group_count = lax.axis_size("grp")
    antenna_row_set = voltages.shape[0]
    samples = voltages.shape[1]
    filter_tap_count = filter_taps.shape[0]
    frame_length = filter_taps.shape[1]
    channel_spectra = samples // frame_length
    channels = frame_length // 2
    antennas = antenna_of_row.shape[0]
    beam_count = beam_weights.shape[2]
    past_samples = shifted(
        voltages[:, samples - (filter_tap_count - 1) * frame_length :], "section", 1
    )
    extended = jnp.concatenate([past_samples, voltages], axis=1).reshape(
        antenna_row_set, channel_spectra + filter_tap_count - 1, frame_length
    )
    weighted = filter_taps[0] * extended[:, 0:channel_spectra, :]
    for tap_index in range(1, filter_tap_count):
        weighted = (
            weighted
            + filter_taps[tap_index] * extended[:, tap_index : tap_index + channel_spectra, :]
        )
    weighted = weighted.astype(jnp.bfloat16)
    split_ways = 1
    dft_cols = dft_table(frame_length, group_count, split_ways)
    channelised = jnp.einsum(
        "asp,pj->ajs", weighted, dft_cols, preferred_element_type=jnp.float32
    ).astype(jnp.bfloat16)[None]
    per_target = channels // (group_count * split_ways)
    ordered = jnp.take(beam_weights, antenna_of_row, axis=3).reshape(
        per_target, 2 * beam_count, antennas
    )
    tables = block_tables(DFT_LEN)
    received = lax.all_to_all(channelised, "grp", split_axis=2, concat_axis=0, tiled=True)
    item_count = received.shape[3]
    halves = received.shape[0] * received.shape[1] // antennas
    all_rows = received.reshape(halves, antennas, 2 * per_target, item_count)
    with_real = jnp.einsum(
        "cba,hacs->cbhs",
        ordered,
        all_rows[:, :, :per_target, :],
        preferred_element_type=jnp.float32,
    )
    with_imag = jnp.einsum(
        "cba,hacs->cbhs",
        ordered,
        all_rows[:, :, per_target:, :],
        preferred_element_type=jnp.float32,
    )
    beam_real = with_real[:, :beam_count] - with_imag[:, beam_count:]
    beam_imag = with_imag[:, :beam_count] + with_real[:, beam_count:]
    formed = jnp.stack([beam_real, beam_imag], axis=1).astype(jnp.bfloat16)
    arrival_buffer = lax.all_to_all(
        formed.reshape(per_target, 2, beam_count, channel_spectra),
        "grp",
        split_axis=2,
        concat_axis=0,
        tiled=True,
    )
    leading = shifted(arrival_buffer[:, :, :, channel_spectra - DFT_LEN // 2 :], "section", 1)
    result = dedisperse(arrival_buffer, leading, beam_delay, tables, channels)
    return result


def solution(mesh):
    in_specs = (P("grp", "section"), P(), P("grp", None, None, None), P(), P("grp"))
    out_specs = P(None, None, "grp", "section")
    return jax.shard_map(local, mesh=mesh, in_specs=in_specs, out_specs=out_specs, check_vma=False)
```

profile of v0, /device:TPU:0, one launch (start us, length us, event | category | flops | bytes accessed | tf_op | source)
XLA Modules:
  0.0 1976.4 jit_solution(12122899857164129571)
XLA Ops:
  15.7 23.4 %pad_maximum_fusion = bf16[64,265728]{1,0:T(8,128)(2,1)} fusion(bf16[64,262144]{1,0:T(8,128)(2,1)} %param.5, bf16[64,3584]{1,0:T(8,128)(2,1)S(1)} %collective-permute-done), kind=kLoop, calls=%fused_computation.2 | loop fusion | flops 68026368 | bytes 68026368 | tf_op jit(solution)/shard_map/concatenate | solution.py:112
  39.1 49.5 %reshape.188 = bf16[64,519,512]{2,1,0:T(8,128)(2,1)} reshape(bf16[64,265728]{1,0:T(8,128)(2,1)} %pad_maximum_fusion) | data formatting | bytes 68026368 | tf_op jit(solution)/shard_map/reshape | solution.py:112
  88.5 127.1 %convert_bitcast_fusion = bf16[1,64,512,512]{3,2,1,0:T(8,128)(2,1)} fusion(bf16[64,519,512]{2,1,0:T(8,128)(2,1)} %reshape.188, f32[512]{0:T(512)S(1)} %bitcast.102, f32[512]{0:T(512)S(1)} %bitcast.103, f32[512]{0:T(512)S(1)} %bitcast.97, f32[512]{0:T(512)S(1)} %bitcast.98, f32[512]{0:T(512)S(1)} %bitcast.99, f32[512]{0:T(512)S(1)} %bitcast.100, ...), kind=kOutput, calls=%fused_computation.9 | convolution fusion | flops 17599299584 | bytes 302530560 | tf_op jit(solution)/shard_map/asp,pj->ajs/dot_general | solution.py:124
  215.7 31.1 %copy.46 = bf16[1,64,512,512]{3,1,0,2:T(8,128)(2,1)} copy(bf16[1,64,512,512]{3,2,1,0:T(8,128)(2,1)} %convert_bitcast_fusion) | data formatting | bytes 67108864 | tf_op jit(solution)/shard_map/broadcast_in_dim | solution.py:124
  253.0 46.1 %copy.44 = bf16[16,2,512,1024]{2,0,1,3:T(8,128)(2,1)} copy(bf16[16,2,512,1024]{3,2,1,0:T(8,128)(2,1)} %param.7) | data formatting | bytes 67108864 | tf_op args[2]
  299.1 35.5 %gather_fusion = bf16[1024,16,2,512]{3,1,2,0:T(8,128)(2,1)} fusion(bf16[16,2,512,1024]{2,0,1,3:T(8,128)(2,1)} %copy.44, s32[1024]{0:T(1024)S(1)} %fusion.55), kind=kCustom, calls=%fused_computation | custom fusion | bytes 67112960 | tf_op jit(solution)/shard_map/jit(_take)/gather | solution.py:128
  334.6 44.9 %copy.45 = bf16[16,2,512,1024]{3,2,1,0:T(8,128)(2,1)} copy(bf16[16,2,512,1024]{2,0,1,3:T(8,128)(2,1)} %bitcast.88) | data formatting | bytes 67108864 | tf_op jit(solution)/shard_map/jit(_take)/gather | solution.py:128
  379.6 23.3 %bitcast_select_fusion = bf16[16,1024,1024]{2,1,0:T(8,128)(2,1)} fusion(bf16[16,2,512,1024]{3,2,1,0:T(8,128)(2,1)} %copy.45, pred[1024]{0:T(1024)(128)(4,1)S(1)} %compare_and_fusion), kind=kLoop, calls=%fused_computation.6 | loop fusion | flops 16777216 | bytes 67109888 | tf_op jit(solution)/shard_map/jit(_take)/select_n | solution.py:128
  402.9 439.0 %all-to-all-done = bf16[1,64,512,512]{3,1,0,2:T(8,128)(2,1)} async-done(((bf16[1,64,512,512]{3,1,0,2:T(8,128)(2,1)}), bf16[1,64,512,512]{3,1,0,2:T(8,128)(2,1)}, u32[]{:S(2)}, u32[]{:S(2)}) %all-to-all-start) | async-done | bytes 33554464 | tf_op jit(solution)/shard_map/all_to_all | solution.py:132
  841.9 22.9 %copy.47 = bf16[1,64,16,32,512]{4,1,2,3,0:T(8,128)(2,1)} copy(bf16[1,64,16,32,512]{4,1,3,2,0:T(8,128)(2,1)} %bitcast.13) | data formatting | bytes 67108864 | tf_op jit(solution)/shard_map/all_to_all | solution.py:132
  864.8 34.4 %fusion.18 = f32[16,1024,1,512]{3,1,0,2:T(8,128)} fusion(bf16[16,1024,1024]{2,1,0:T(8,128)(2,1)} %bitcast_select_fusion, bf16[1,1024,32,512]{3,1,2,0:T(8,128)(2,1)} %bitcast.94), kind=kOutput, calls=%fused_computation.34 | convolution fusion | flops 17179869184 | bytes 83886080 | tf_op jit(solution)/shard_map/cba,hacs->cbhs/dot_general | solution.py:136
  899.2 34.4 %fusion.19 = f32[16,1024,1,512]{3,1,0,2:T(8,128)} fusion(bf16[16,1024,1024]{2,1,0:T(8,128)(2,1)} %bitcast_select_fusion, bf16[1,1024,32,512]{3,1,2,0:T(8,128)(2,1)} %bitcast.95), kind=kOutput, calls=%fused_computation.35 | convolution fusion | flops 17179869184 | bytes 83886080 | tf_op jit(solution)/shard_map/cba,hacs->cbhs/dot_general | solution.py:142
  933.5 25.5 %fusion.21 = (bf16[16,1,512,512]{3,2,0,1:T(8,128)(2,1)S(1)}, bf16[16,1,512,512]{3,2,0,1:T(8,128)(2,1)}) fusion(f32[16,1024,1,512]{3,1,0,2:T(8,128)} %fusion.19, f32[16,1024,1,512]{3,1,0,2:T(8,128)} %fusion.18), kind=kLoop, calls=%fused_computation.37 | loop fusion | flops 16777216 | bytes 83886080 | tf_op jit(solution)/shard_map/stack | solution.py:150
  965.3 24.7 %copy.48 = bf16[16,2,512,512]{3,0,1,2:T(8,128)(2,1)S(1)} copy(bf16[16,2,512,512]{3,2,0,1:T(8,128)(2,1)S(1)} %pad_maximum_fusion.4) | data formatting | bytes 33554432 | tf_op jit(solution)/shard_map/stack | solution.py:150
  990.1 509.1 %all_to_all.33 = bf16[16,2,512,512]{3,0,1,2:T(8,128)(2,1)} all-to-all(bf16[16,2,512,512]{3,0,1,2:T(8,128)(2,1)S(1)} %copy.48), channel_id=1, replica_groups=mesh['section'=2,'grp'=16] {'grp'}, dimensions={2} | all-to-all | bytes 33554432 | tf_op jit(solution)/shard_map/all_to_all | solution.py:151
  1523.6 31.9 %fusion.24 = (f32[256,32,256]{2,0,1:T(8,128)}, f32[256,32,256]{2,0,1:T(8,128)}) fusion(f32[256]{0:T(256)S(1)} %get-tuple-element.26, f32[256]{0:T(256)S(1)} %get-tuple-element.25, f32[256,32]{0,1:T(8,128)S(1)} %broadcast_multiply_fusion), kind=kLoop, calls=%fused_computation.41 | loop fusion | flops 4194304 | bytes 16812032 | tf_op jit(solution)/shard_map/cos | solution.py:66
  1555.6 55.6 %collective-permute-done.1 = bf16[256,2,32,128]{3,2,1,0:T(8,128)(2,1)S(1)} collective-permute-done((bf16[256,2,32,128]{3,2,1,0:T(8,128)(2,1)S(1)}, bf16[256,2,32,128]{3,2,1,0:T(8,128)(2,1)S(1)}, u32[]{:S(2)}, u32[]{:S(2)}) %collective-permute-start.1) | collective-permute-done | bytes 4194336 | tf_op jit(solution)/shard_map/ppermute | solution.py:14
  1623.3 29.9 %copy.51 = bf16[256,2,32,640]{0,3,2,1:T(8,128)(2,1)} copy(bf16[256,2,32,640]{3,2,1,0:T(8,128)(2,1)} %pad_maximum_fusion.2) | data formatting | bytes 41943040 | tf_op jit(solution)/shard_map/concatenate | solution.py:77
  1653.2 23.4 %fusion.85 = (bf16[256,2,32,4,128]{0,4,3,2,1:T(8,128)(2,1)}, bf16[256,2,32,4,128]{0,4,3,2,1:T(8,128)(2,1)}) fusion(bf16[256,2,32,5,128]{0,4,3,2,1:T(8,128)(2,1)} %bitcast.87), kind=kLoop, calls=%fused_computation.139 | loop fusion | bytes 67108864 | tf_op jit(solution)/shard_map/slice | solution.py:80
  1719.0 28.9 %fusion.5 = f32[256,32,4,512]{3,0,2,1:T(8,128)} fusion(bf16[256,2,32,4,128]{4,0,3,2,1:T(8,128)(2,1)} %copy.65, bf16[256,2,32,4,128]{4,0,3,2,1:T(8,128)(2,1)} %copy.66, bf16[256,256]{1,0:T(8,128)(2,1)S(1)} %fusion.54, bf16[256,256]{1,0:T(8,128)(2,1)S(1)} %get-tuple-element.24), kind=kOutput, calls=%fused_computation.17 | convolution fusion | flops 8624013312 | bytes 100925440 | tf_op jit(solution)/shard_map/cbml,lk->cbmk/dot_general | solution.py:81
  1747.9 50.8 %convolution_add_fusion = f32[256,32,4,512]{3,0,2,1:T(8,128)} fusion(f32[256,32,4,512]{3,0,2,1:T(8,128)} %fusion.5, bf16[256,2,32,4,128]{4,0,3,2,1:T(8,128)(2,1)} %copy.66, bf16[256,2,32,4,128]{4,0,3,2,1:T(8,128)(2,1)} %copy.65, bf16[256,256]{1,0:T(8,128)(2,1)S(1)} %get-tuple-element.24, bf16[256,256]{1,0:T(8,128)(2,1)S(1)} %get-tuple-element.23), kind=kOutput, calls=%fused_computation.11 | convolution fusion | flops 8640790528 | bytes 168034304 | tf_op jit(solution)/shard_map/cbml,lk->cbmk/dot_general | solution.py:83
  1798.7 40.6 %fusion.1 = f32[256,32,4,256]{0,3,2,1:T(8,128)} fusion(f32[256,32,4,512]{3,0,2,1:T(8,128)} %convolution_add_fusion, f32[256,32,256]{2,0,1:T(8,128)} %get-tuple-element.14, f32[256,32,256]{2,0,1:T(8,128)} %get-tuple-element.13, bf16[256,128]{1,0:T(8,128)(2,1)S(1)} %get-tuple-element.12, bf16[256,128]{1,0:T(8,128)(2,1)S(1)} %slice.163), kind=kOutput, calls=%fused_computation.13 | convolution fusion | flops 4328783872 | bytes 117571584 | tf_op jit(solution)/shard_map/cbmk,kn->cbmn/dot_general | solution.py:91
  1839.3 50.3 %fusion.20 = f32[256,32,4,256]{0,3,2,1:T(8,128)} fusion(f32[256,32,4,256]{0,3,2,1:T(8,128)} %fusion.1, f32[256,32,4,512]{3,0,2,1:T(8,128)} %convolution_add_fusion, f32[256,32,256]{2,0,1:T(8,128)} %get-tuple-element.14, f32[256,32,256]{2,0,1:T(8,128)} %get-tuple-element.13, bf16[256,128]{1,0:T(8,128)(2,1)S(1)} %slice.163, bf16[256,128]{1,0:T(8,128)(2,1)S(1)} %copy-done), kind=kOutput, calls=%fused_computation.36 | convolution fusion | flops 4337172480 | bytes 151126016 | tf_op jit(solution)/shard_map/cbmk,kn->cbmn/dot_general | solution.py:93
  1951.6 24.6 %pad_maximum_fusion.1 = f32[256,2,32,512]{3,2,1,0:T(8,128)} fusion(f32[256,1,32,512]{3,2,1,0:T(8,128)} %copy.57, f32[256,1,32,512]{3,2,1,0:T(8,128)} %copy.56), kind=kLoop, calls=%fused_computation.5 | loop fusion | flops 8388608 | bytes 67108864 | tf_op jit(solution)/shard_map/stack | solution.py:96
  (34 shorter events, 169.1 us)
Async XLA Ops:
  1.1 14.6 collective-permute-start
  246.7 595.1 %all-to-all-start = ((bf16[1,64,512,512]{3,1,0,2:T(8,128)(2,1)}), bf16[1,64,512,512]{3,1,0,2:T(8,128)(2,1)}, u32[]{:S(2)}, u32[]{:S(2)}) async-start(bf16[1,64,512,512]{3,1,0,2:T(8,128)(2,1)} %copy.46), calls=%async_computation | async-start | bytes 67108864 | tf_op jit(solution)/shard_map/all_to_all | solution.py:132
  253.0 46.1 %copy-start.1 = (s32[1024]{0:T(1024)S(1)}, s32[1024]{0:T(1024)}, u32[]{:S(2)}) copy-start(s32[1024]{0:T(1024)} %param.8) | copy-start | bytes 12292
  990.0 532.8 %copy-start.2 = (s32[32]{0:T(128)S(1)}, s32[32]{0:T(128)}, u32[]{:S(2)}) copy-start(s32[32]{0:T(128)} %param.9) | copy-start | bytes 388
  1516.1 95.1 %collective-permute-start.1 = (bf16[256,2,32,128]{3,2,1,0:T(8,128)(2,1)S(1)}, bf16[256,2,32,128]{3,2,1,0:T(8,128)(2,1)S(1)}, u32[]{:S(2)}, u32[]{:S(2)}) collective-permute-start(bf16[256,2,32,128]{3,2,1,0:T(8,128)(2,1)S(1)} %slice.156), channel_id=1, source_target_pairs={{0,16},{1,17},{2,18},{3,19},{4,20},{5,21},{6,22},{7,23},{8,24},{9,... | collective-permute-start | bytes 12582920 | tf_op jit(solution)/shard_map/ppermute | solution.py:14
  1798.7 40.7 %copy-start = (bf16[256,128]{1,0:T(8,128)(2,1)S(1)}, bf16[256,128]{1,0:T(8,128)(2,1)}, u32[]{:S(2)}) copy-start(bf16[256,128]{1,0:T(8,128)(2,1)} %get-tuple-element.11) | copy-start | bytes 196612
where the time goes:
time: 1990 us; the launch traced here: 1980 us
  blocking collectives  509 us (26%)
  waiting for transfers between devices  498 us (25%)
  local copies, waits for them, and re-layouts  431 us (22%)
  matrix products  367 us (18%)
  other arithmetic  155 us (8%)
    all_to_all x1, blocking collectives, local(): lax.all_to_all(formed.reshape(per_target, 2, beam_count, channel_spectra)...  509 us
    all_to_all x1, waiting for transfers between devices, local(): lax.all_to_all(channelised, 'grp', split_axis=2, concat_axis=0, tiled=True)  439 us
    dot_general x1, matrix products, local(): jnp.einsum('asp,pj->ajs', weighted, dft_cols, preferred_element_type=jnp....  127 us
    unnamed x9, local copies, waits for them, and re-layouts  88.6 us
    gather x2, local copies, waits for them, and re-layouts, local(): jnp.take(beam_weights, antenna_of_row, axis=3)  80.5 us
    ppermute x2, waiting for transfers between devices, shifted(): lax.ppermute(value, axis, [(source, source + steps) for source in range(l...  59.2 us
    dot_general x1, matrix products, dedisperse(): jnp.einsum('cbml,lk->cbmk', blocks[:, 1], forward_imag, preferred_element...  50.8 us
    dot_general x1, matrix products, dedisperse(): jnp.einsum('cbmk,kn->cbmn', filtered_imag, inverse_imag, preferred_elemen...  50.3 us
  transfers between devices with their start and end apart: 3, of which 3 were waited for; matrix products, arithmetic and copies ran while one was open for 10% of the time, Pallas kernels for 0%

commit v1 on v0

v1 whole, which is shorter than its diff:
```python
import functools
import math

import jax
import jax.numpy as jnp
import numpy as np
from jax import lax
from jax.experimental import pallas as pl
from jax.experimental.pallas import tpu as pltpu
from jax.sharding import PartitionSpec as P

DFT_LEN = 256
GAP = 8
ANTENNA_BLOCK = 16
VMEM_LIMIT = 56 * 1024 * 1024


def shifted(value, axis, steps):
    count = lax.axis_size(axis)
    leading, last = (max(0, -steps), min(count, count - steps))
    return lax.ppermute(value, axis, [(source, source + steps) for source in range(leading, last)])


def dft_rows(frame_length, group_count):
    channels = frame_length // 2
    per_target = channels // group_count
    row = np.arange(frame_length)
    target = row // (2 * per_target)
    within = row % (2 * per_target)
    quadrature = within // per_target
    channel = target * per_target + within % per_target
    winding = np.arange(frame_length)[None, :] * channel[:, None] % frame_length
    angles = np.float32(2.0 * math.pi / frame_length) * winding.astype(np.float32)
    factor = np.float32(channels ** (-0.5))
    table = np.where(quadrature[:, None] == 0, np.cos(angles) * factor, -np.sin(angles) * factor)
    return jnp.asarray(table.astype(jnp.bfloat16))


def block_tables(length):
    half_len = length // 2
    factor = length ** (-0.5)
    sample = jnp.arange(length, dtype=jnp.int32)
    angles = (
        2.0 * math.pi / length * (sample[:, None] * sample[None, :] % length).astype(jnp.float32)
    )
    cosine_table = (jnp.cos(angles) * factor).astype(jnp.bfloat16)
    sine_table = (jnp.sin(angles) * factor).astype(jnp.bfloat16)
    forward_real = jnp.concatenate([cosine_table, -sine_table], axis=1)
    forward_imag = jnp.concatenate([sine_table, cosine_table], axis=1)
    back_cos = cosine_table[:, half_len:]
    back_sin = sine_table[:, half_len:]
    inverse_real = jnp.concatenate([back_cos, back_sin], axis=1)
    inverse_imag = jnp.concatenate([-back_sin, back_cos], axis=1)
    return (forward_real, forward_imag, inverse_real, inverse_imag)


def chirp_factor(delays, channel_count, channels, length):
    frequency = jnp.arange(length, dtype=jnp.int32)
    signed = jnp.where(frequency < length // 2, frequency, frequency - length).astype(jnp.float32)
    channel = jnp.arange(channel_count, dtype=jnp.int32).astype(jnp.float32)
    strength = (1.0 + channel / channels) ** (-3.0)
    sweep = signed * signed / (length * length)
    phases = (math.pi * delays.astype(jnp.float32))[None, :, None] * strength[
        :, None, None
    ] * sweep[None, None, :] - 0.5 * math.pi * frequency.astype(jnp.float32)[None, None, :]
    return (jnp.cos(phases), jnp.sin(phases))


def channelise_kernel(taps, frame, spectra, edge, *refs):
    taps_ref, table_ref, past_ref, now_ref = refs[:4]
    out_ref, w_ref, x_ref = refs[-3:]
    rows = now_ref.shape[0]
    past_frames = past_ref.shape[1] // frame
    group = 8
    lanes = 128
    at_edge = pl.program_id(0) == 0

    def filter_group(frames, first, lane):
        weights = [
            jnp.broadcast_to(taps_ref[k : k + 1, lane : lane + lanes], (8, lanes))
            for k in range(taps)
        ]
        for half in range(rows // 8):
            part = [f[half * 8 : half * 8 + 8] for f in frames]
            for i in range(group):
                total = weights[0] * part[i]
                for k in range(1, taps):
                    total = total + weights[k] * part[i + k]
                at = pl.multiple_of((first + i) * (rows + GAP) + half * 8, 8)
                w_ref[lane // lanes, pl.ds(at, 8), :] = total

    def earlier(start):
        value = past_ref[:, start : start + lanes]
        if edge:
            value = jnp.where(at_edge, refs[4][:, start : start + lanes], value)
        return value

    for lane in range(0, frame, lanes):
        frames = []
        for i in range(1 - taps, group):
            if i < 0:
                value = earlier((i + past_frames) * frame + lane)
            else:
                value = now_ref[:, i * frame + lane : i * frame + lane + lanes]
            frames.append(value.astype(jnp.float32))
        filter_group(frames, 0, lane)

    def later(step, carry):
        for lane in range(0, frame, lanes):
            frames = []
            for i in range(1 - taps, group):
                start = pl.multiple_of((step * group + i) * frame + lane, lanes)
                frames.append(now_ref[:, pl.ds(start, lanes)].astype(jnp.float32))
            filter_group(frames, step * group, lane)
        return carry

    lax.fori_loop(1, spectra // group, later, 0)

    def transform(pair, carry):
        parts = []
        for i in range(2):
            row = [
                w_ref[lane, pl.ds(pair * 2 + i, spectra, stride=rows + GAP), :].astype(jnp.bfloat16)
                for lane in range(frame // lanes)
            ]
            parts.append(jnp.concatenate(row, axis=1))
        both = jnp.concatenate(parts, axis=0)
        result = lax.dot_general(
            table_ref[...], both, (((1,), (1,)), ((), ())), preferred_element_type=jnp.float32
        )
        for i in range(2):
            at = pl.multiple_of((pair * 2 + i) * (frame + GAP), GAP)
            x_ref[pl.ds(at, frame), :] = result[:, i * spectra : (i + 1) * spectra]
        return carry

    lax.fori_loop(0, rows // 2, transform, 0, unroll=4)

    def arrange(step, carry):
        for i in range(8):
            j = step * 8 + i
            out_ref[j] = x_ref[pl.ds(j, rows, stride=frame + GAP), :].astype(jnp.bfloat16)
        return carry

    lax.fori_loop(0, frame // 8, arrange, 0)


def channelise(voltages, halo, filter_taps, table, first, count, spectra, low, high):
    taps, frame = filter_taps.shape
    rows = ANTENNA_BLOCK
    past_frames = halo.shape[1] // frame
    per_block = spectra // past_frames
    base = low // rows
    edge = first == 0
    operands = [filter_taps, table, voltages, voltages]
    specs = [
        pl.BlockSpec((taps, frame), lambda t, a: (0, 0)),
        pl.BlockSpec((frame, frame), lambda t, a: (0, 0)),
        pl.BlockSpec(
            (rows, past_frames * frame),
            lambda t, a: (base + a, jnp.maximum((first + t) * per_block - 1, 0)),
        ),
        pl.BlockSpec((rows, spectra * frame), lambda t, a: (base + a, first + t)),
    ]
    if edge:
        operands.append(halo)
        specs.append(pl.BlockSpec((rows, past_frames * frame), lambda t, a: (base + a, 0)))
    return pl.pallas_call(
        functools.partial(channelise_kernel, taps, frame, spectra, edge),
        grid=(count, (high - low) // rows),
        in_specs=specs,
        out_specs=pl.BlockSpec((frame, rows, spectra), lambda t, a: (0, a, t)),
        out_shape=jax.ShapeDtypeStruct((frame, high - low, count * spectra), jnp.bfloat16),
        scratch_shapes=[
            pltpu.VMEM((frame // 128, (spectra + 1) * (rows + GAP), 128), jnp.float32),
            pltpu.VMEM(((rows + 1) * (frame + GAP), spectra), jnp.float32),
        ],
        compiler_params=pltpu.CompilerParams(vmem_limit_bytes=VMEM_LIMIT),
        cost_estimate=pl.CostEstimate(
            flops=4 * count * (high - low) * spectra * frame * frame,
            bytes_accessed=4 * count * (high - low) * spectra * frame,
            transcendentals=0,
        ),
        name="channelise",
    )(*operands)


def beamform_kernel(cuts, weights_ref, *refs):
    out_ref = refs[-1]
    inputs = refs[:-1]
    groups = out_ref.shape[0]
    spectra = out_ref.shape[-1]
    beams = weights_ref.shape[2]

    def rows_of(quadrature):
        parts = []
        for ref in inputs[quadrature::2]:
            bounds = [0] + (cuts if len(inputs) == 2 else []) + [ref.shape[2]]
            for low, high in zip(bounds[:-1], bounds[1:]):
                parts.append(ref[:, 0, low:high, :].reshape(groups * (high - low), spectra))
        return parts[0] if len(parts) == 1 else jnp.concatenate(parts, axis=0)

    both = jnp.concatenate([rows_of(0), rows_of(1)], axis=1)
    share = beams // groups
    step = max(share, 128)
    for first in range(0, beams, step):
        by_real = jnp.dot(
            weights_ref[0, 0, first : first + step], both, preferred_element_type=jnp.float32
        )
        by_imag = jnp.dot(
            weights_ref[0, 1, first : first + step], both, preferred_element_type=jnp.float32
        )
        beam_real = (by_real[:, :spectra] - by_imag[:, spectra:]).astype(jnp.bfloat16)
        beam_imag = (by_real[:, spectra:] + by_imag[:, :spectra]).astype(jnp.bfloat16)
        low = first // share
        high = low + step // share
        out_ref[low:high, 0, 0] = beam_real.reshape(step // share, share, spectra)
        out_ref[low:high, 0, 1] = beam_imag.reshape(step // share, share, spectra)


def beamform(weights, received, cuts, first, count, spectra, low, high):
    per_target, _, beams, antennas = weights.shape
    groups = received[0].shape[0]
    share = beams // groups
    specs = [pl.BlockSpec((1, 2, beams, antennas), lambda c, t: (low + c, 0, 0, 0))]
    operands = [weights]
    for array in received:
        block = (groups, 1, array.shape[2], spectra)
        specs.append(pl.BlockSpec(block, lambda c, t: (0, low + c, 0, first + t)))
        specs.append(pl.BlockSpec(block, lambda c, t: (0, per_target + low + c, 0, first + t)))
        operands += [array, array]
    return pl.pallas_call(
        functools.partial(beamform_kernel, cuts),
        grid=(high - low, count),
        in_specs=specs,
        out_specs=pl.BlockSpec((groups, 1, 2, share, spectra), lambda c, t: (0, c, 0, 0, t)),
        out_shape=jax.ShapeDtypeStruct(
            (groups, high - low, 2, share, count * spectra), jnp.bfloat16
        ),
        compiler_params=pltpu.CompilerParams(vmem_limit_bytes=VMEM_LIMIT),
        cost_estimate=pl.CostEstimate(
            flops=8 * (high - low) * beams * antennas * spectra * count,
            bytes_accessed=4 * (high - low) * beams * (antennas + 2 * spectra * count),
            transcendentals=0,
        ),
        name="beamform",
    )(*operands)


def dedisperse_kernel(count, *refs):
    pieces = refs[: count + 1]
    cos_ref, sin_ref, fr_ref, fi_ref, ir_ref, ii_ref = refs[count + 1 : count + 7]
    out_ref = refs[-1]
    sources, chans, _, beams, advance = pieces[0].shape
    length = 2 * advance
    merged = sources * chans * beams
    chirp_real = cos_ref[...].reshape(merged, length)
    chirp_imag = sin_ref[...].reshape(merged, length)

    def part(ref, quadrature):
        return ref[:, :, quadrature].reshape(merged, advance)

    for m in range(count):
        before, after = pieces[m], pieces[m + 1]
        real = jnp.concatenate([part(before, 0), part(after, 0)], axis=1)
        imag = jnp.concatenate([part(before, 1), part(after, 1)], axis=1)
        spectrum = jnp.dot(real, fr_ref[...], preferred_element_type=jnp.float32) + jnp.dot(
            imag, fi_ref[...], preferred_element_type=jnp.float32
        )
        spec_real = spectrum[:, :length]
        spec_imag = spectrum[:, length:]
        filtered_real = (spec_real * chirp_real - spec_imag * chirp_imag).astype(jnp.bfloat16)
        filtered_imag = (spec_real * chirp_imag + spec_imag * chirp_real).astype(jnp.bfloat16)
        result = jnp.dot(filtered_real, ir_ref[...], preferred_element_type=jnp.float32) + jnp.dot(
            filtered_imag, ii_ref[...], preferred_element_type=jnp.float32
        )
        at = slice(m * advance, (m + 1) * advance)
        out_ref[:, :, 0, :, at] = result[:, :advance].reshape(sources, chans, beams, advance)
        out_ref[:, :, 1, :, at] = result[:, advance:].reshape(sources, chans, beams, advance)


def dedisperse(pieces, first, blocks, low, high, chans, chirp, tables, output):
    count = len(pieces) - 1
    groups, per_target, beams, length = chirp[0].shape
    advance = length // 2
    sources = max(1, min(groups, 1024 // (beams * chans)))

    def piece_spec(block, start):
        skip = (low - start) // chans
        return pl.BlockSpec(
            (sources, chans, 2, beams, advance), lambda g, c: (g, skip + c, 0, 0, block)
        )

    base = low // chans
    factor = pl.BlockSpec((sources, chans, beams, length), lambda g, c: (g, base + c, 0, 0))
    specs = [piece_spec(block, start) for _, block, start in pieces] + [factor] * 2
    specs += [pl.BlockSpec(t.shape, lambda g, c: (0, 0)) for t in tables]
    operands = [array for array, _, _ in pieces] + list(chirp) + list(tables)
    aliases = {}
    if output is not None:
        aliases = {len(operands): 0}
        operands.append(output)
        specs.append(pl.BlockSpec(memory_space=pl.ANY))
    return pl.pallas_call(
        functools.partial(dedisperse_kernel, count),
        grid=(groups // sources, (high - low) // chans),
        in_specs=specs,
        out_specs=pl.BlockSpec(
            (sources, chans, 2, beams, count * advance),
            lambda g, c: (g, base + c, 0, 0, first // count),
        ),
        out_shape=jax.ShapeDtypeStruct(
            (groups, per_target, 2, beams, blocks * advance), jnp.float32
        ),
        input_output_aliases=aliases,
        compiler_params=pltpu.CompilerParams(vmem_limit_bytes=VMEM_LIMIT),
        cost_estimate=pl.CostEstimate(
            flops=12 * count * groups * (high - low) * beams * length * length,
            bytes_accessed=groups * (high - low) * beams * advance * (12 * count + 20),
            transcendentals=0,
        ),
        name="dedisperse",
    )(*operands)


def local(voltages, filter_taps, beam_weights, antenna_of_row, beam_delay):
    group_count = lax.axis_size("grp")
    antenna_rows, samples = voltages.shape
    taps, frame = filter_taps.shape
    spectra = samples // frame
    channels = frame // 2
    antennas = antenna_of_row.shape[0]
    per_target = channels // group_count
    advance = DFT_LEN // 2
    blocks = spectra // advance
    last = blocks - 1

    table = dft_rows(frame, group_count)
    past_frames = -(-(taps - 1) // 8) * 8
    halo = shifted(voltages[:, samples - past_frames * frame :], "section", 1)

    cut = ANTENNA_BLOCK
    cuts = [cut] if cut < antenna_rows else []
    bounds = [0] + cuts + [antenna_rows]
    row_order = np.concatenate(
        [
            (np.arange(group_count)[:, None] * antenna_rows + np.arange(low, high)[None, :]).ravel()
            for low, high in zip(bounds[:-1], bounds[1:])
        ]
    )
    chosen = (
        jnp.arange(antennas, dtype=jnp.int32)[:, None] == antenna_of_row[row_order][None, :]
    ).astype(jnp.bfloat16)
    ordered = jnp.einsum(
        "ckba,ar->ckbr", beam_weights, chosen, preferred_element_type=jnp.float32
    ).astype(jnp.bfloat16)
    tables = block_tables(DFT_LEN)
    chirp = chirp_factor(beam_delay, channels, channels, DFT_LEN)
    chirp = tuple(c.reshape((group_count, per_target) + c.shape[1:]) for c in chirp)

    previous = None

    def exchange(value, previous):
        if previous is not None:
            value, previous = lax.optimization_barrier((value, previous))
        return lax.all_to_all(value, "grp", split_axis=0, concat_axis=0, tiled=True)

    def send_spectra(first, count, low, high, previous):
        value = channelise(voltages, halo, filter_taps, table, first, count, advance, low, high)
        value = value.reshape(group_count, 2 * per_target, high - low, count * advance)
        return exchange(value, previous)

    received_last = []
    for low, high in zip(bounds[:-1], bounds[1:]):
        previous = send_spectra(last, 1, low, high, previous)
        received_last.append(previous)
    received_rest = previous = send_spectra(0, last, 0, antenna_rows, previous)

    form = functools.partial(beamform, ordered)
    whole = (0, per_target)
    value = form(received_last, cuts, 0, 1, advance, *whole)
    value, chirp = lax.optimization_barrier((value, chirp))
    series_last = previous = exchange(value, previous)
    leading = shifted(series_last, "section", 1)
    value = form([received_rest], cuts, 0, last - 1, advance, *whole)
    series_early = previous = exchange(value, previous)

    tail = max(1, per_target // 4)
    middle = per_target - tail
    value = form([received_rest], cuts, last - 1, 1, advance, 0, middle)
    value, leading = lax.optimization_barrier((value, leading))
    series_head = previous = exchange(value, previous)
    value = form([received_rest], cuts, last - 1, 1, advance, middle, per_target)
    early = [(leading, 0, 0)] + [(series_early, m, 0) for m in range(last - 1)]
    output = dedisperse(early, 0, blocks, 0, per_target, tail, chirp, tables, None)
    value, output = lax.optimization_barrier((value, output))
    series_tail = exchange(value, previous)

    before, after = (series_early, last - 2, 0), (series_last, 0, 0)
    for low, high, series in ((0, middle, series_head), (middle, per_target, series_tail)):
        pieces = [before, (series, 0, low), after]
        output = dedisperse(pieces, last - 1, blocks, low, high, tail, chirp, tables, output)
    return output.reshape((channels,) + output.shape[2:])


def solution(mesh):
    in_specs = (P("grp", "section"), P(), P("grp", None, None, None), P(), P("grp"))
    out_specs = P(None, None, "grp", "section")
    return jax.shard_map(local, mesh=mesh, in_specs=in_specs, out_specs=out_specs, check_vma=False)
```

time: 1990 us -> 1150 us (0.58)
  blocking collectives: 509 us -> 0 us
  local copies, waits for them, and re-layouts: 431 us -> 6.44 us
  matrix products: 367 us -> 43.5 us
  Pallas kernels: 0 us -> 230 us
  starting transfers between devices: 15.8 us -> 231 us
  other arithmetic: 155 us -> 35.7 us
  waiting for transfers between devices: 498 us -> 600 us
    all_to_all x1 -> x0, blocking collectives: 509 us -> none  [local(): lax.all_to_all(formed.reshape(per_target, 2, beam_count, channel_spectra)...]
    dot_general x7 -> x1, matrix products: 367 us -> 43.5 us  [local(): jnp.einsum('ckba,ar->ckbr', beam_weights, chosen, preferred_element_type=...]
    pallas_call x0 -> x10, Pallas kernels: none -> 230 us  [the longest x3 91.2 us: channelise(): pl.pallas_call(functools.partial(channelise_kernel, taps, frame, spectra,...]
    all_to_all x1 -> x7, starting transfers between devices: 6.26 us -> 223 us  [exchange(): return lax.all_to_all(value, 'grp', split_axis=0, concat_axis=0, tiled=True)]
    unnamed x9 -> x14, local copies, waits for them, and re-layouts: 88.6 us -> 0.83 us
    all_to_all x1 -> x7, waiting for transfers between devices: 439 us -> 517 us  [exchange(): return lax.all_to_all(value, 'grp', split_axis=0, concat_axis=0, tiled=True)]
    gather x2 -> x1, local copies, waits for them, and re-layouts: 80.5 us -> 4.53 us  [local(): antenna_of_row[row_order][None, :]]
    another operation x3 -> x0, local copies, waits for them, and re-layouts: 65.2 us -> none  [the longest x2 40.4 us: dedisperse(): return jnp.stack([out_real, out_imag], axis=1)]
  transfers between devices with their start and end apart: 3 -> 9, of which waited for: 3 -> 9; matrix products, arithmetic and copies ran while one was open for 10% -> 7% of each run, Pallas kernels for 0% -> 19%
where the time goes in v1:
time: 1150 us
  waiting for transfers between devices  600 us (52%)
  starting transfers between devices  231 us (20%)
  Pallas kernels  230 us (20%)
  matrix products  43.5 us (4%)
  other arithmetic  35.7 us (3%)
    all_to_all x7, waiting for transfers between devices, exchange(): return lax.all_to_all(value, 'grp', split_axis=0, concat_axis=0, tiled=True)  517 us
    all_to_all x7, starting transfers between devices, exchange(): return lax.all_to_all(value, 'grp', split_axis=0, concat_axis=0, tiled=True)  223 us
    pallas_call x3, Pallas kernels, channelise(): pl.pallas_call(functools.partial(channelise_kernel, taps, frame, spectra,...  91.2 us
    pallas_call x4, Pallas kernels, beamform(): pl.pallas_call(functools.partial(beamform_kernel, cuts), grid=(high - low...  89.6 us
    ppermute x2, waiting for transfers between devices, shifted(): lax.ppermute(value, axis, [(source, source + steps) for source in range(l...  82.9 us
    pallas_call x3, Pallas kernels, dedisperse(): pl.pallas_call(functools.partial(dedisperse_kernel, count), grid=(groups...  49.5 us
    dot_general x1, matrix products, local(): jnp.einsum('ckba,ar->ckbr', beam_weights, chosen, preferred_element_type=...  43.5 us
    sin x1, other arithmetic, chirp_factor(): return (jnp.cos(phases), jnp.sin(phases))  31.9 us
  transfers between devices with their start and end apart: 9, of which 9 were waited for; matrix products, arithmetic and copies ran while one was open for 7% of the time, Pallas kernels for 19%

profile of v1, /device:TPU:0, one launch (start us, length us, event | category | flops | bytes accessed | tf_op | source)
XLA Modules:
  0.0 1147.7 jit_solution(7259577550264812348)
XLA Ops:
  0.0 8.2 channelise.5
  15.6 18.3 %channelise.4 = bf16[512,48,128]{2,1,0:T(8,128)(2,1)} custom-call(f32[8,512]{1,0:T(8,128)} %refs_0_.5, bf16[512,512]{1,0:T(8,128)(2,1)} %constant.48.clone.refs_1_, bf16[64,262144]{1,0:T(8,128)(2,1)} %refs_3_.5, bf16[64,262144]{1,0:T(8,128)(2,1)} %refs_3_.5), custom_call_target="tpu_custom_call" | custom-call | flops 6442450944 | bytes 12582912 | tf_op jit(solution)/shard_map/channelise/pallas_call | solution.py:167
  33.8 22.8 %all-to-all-done.refs_0_.refs_1_ = bf16[16,32,16,128]{3,2,1,0:T(8,128)(2,1)S(1)} async-done(((bf16[16,32,16,128]{3,2,1,0:T(8,128)(2,1)}), bf16[16,32,16,128]{3,2,1,0:T(8,128)(2,1)S(1)}, u32[]{:S(2)}, u32[]{:S(2)}) %all-to-all-start) | async-done | bytes 2097184 | tf_op jit(solution)/shard_map/all_to_all | solution.py:365
  56.7 11.3 all-to-all-start.1
  72.5 11.6 %collective-permute-done.refs_4_ = bf16[64,4096]{1,0:T(8,128)(2,1)S(1)} collective-permute-done((bf16[64,4096]{1,0:T(8,128)(2,1)S(1)}, bf16[64,4096]{1,0:T(8,128)(2,1)S(1)}, u32[]{:S(2)}, u32[]{:S(2)}) %collective-permute-start) | collective-permute-done | bytes 524320 | tf_op jit(solution)/shard_map/ppermute | solution.py:21
  84.9 64.8 %channelise.3 = bf16[512,64,384]{2,1,0:T(8,128)(2,1)} custom-call(f32[8,512]{1,0:T(8,128)} %refs_0_.5, bf16[512,512]{1,0:T(8,128)(2,1)} %constant.48.clone.refs_1_, bf16[64,262144]{1,0:T(8,128)(2,1)} %refs_3_.5, bf16[64,262144]{1,0:T(8,128)(2,1)} %refs_3_.5, bf16[64,4096]{1,0:T(8,128)(2,1)} %copy-done.5), custom_call_target="tpu_custom_call" | custom-call | flops 25769803776 | bytes 50331648 | tf_op jit(solution)/shard_map/channelise/pallas_call | solution.py:167
  149.7 32.4 %all-to-all-done.1.refs_2_.refs_3_ = bf16[16,32,48,128]{3,2,1,0:T(8,128)(2,1)} async-done(((bf16[16,32,48,128]{3,2,1,0:T(8,128)(2,1)}), bf16[16,32,48,128]{3,2,1,0:T(8,128)(2,1)}, u32[]{:S(2)}, u32[]{:S(2)}) %all-to-all-start.1) | async-done | bytes 6291488 | tf_op jit(solution)/shard_map/all_to_all | solution.py:365
  182.1 28.3 %all-to-all-start.2 = ((bf16[16,32,64,384]{3,2,1,0:T(8,128)(2,1)}), bf16[16,32,64,384]{3,2,1,0:T(8,128)(2,1)}, u32[]{:S(2)}, u32[]{:S(2)}) async-start(bf16[16,32,64,384]{3,2,1,0:T(8,128)(2,1)} %bitcast.16), calls=%async_computation.2 | async-start | bytes 50331648 | tf_op jit(solution)/shard_map/all_to_all | solution.py:365
  215.1 31.9 %fusion = (f32[16,16,32,256]{3,2,1,0:T(8,128)}, f32[16,16,32,256]{3,2,1,0:T(8,128)}) fusion(f32[256]{0:T(256)S(1)} %get-tuple-element.40, f32[256]{0:T(256)S(1)} %get-tuple-element.39, f32[16,16,32]{2,1,0:T(8,128)S(1)} %broadcast_multiply_fusion), kind=kLoop, calls=%fused_computation.3 | loop fusion | flops 4194304 | bytes 16812032 | tf_op jit(solution)/shard_map/sin | solution.py:66
  247.0 43.5 %convert_bitcast_fusion.weights_ref = bf16[16,2,512,1024]{3,2,1,0:T(8,128)(2,1)} fusion(bf16[16,2,512,1024]{3,2,1,0:T(8,128)(2,1)} %param.10, s32[1024]{0:T(1024)S(1)} %gather_fusion), kind=kOutput, calls=%fused_computation.1 | convolution fusion | flops 34377564160 | bytes 67112960 | tf_op jit(solution)/shard_map/ckba,ar->ckbr/dot_general | solution.py:353
  290.5 22.7 %beamform.5 = bf16[16,16,2,32,128]{4,3,2,1,0:T(8,128)(2,1)} custom-call(bf16[16,2,512,1024]{3,2,1,0:T(8,128)(2,1)} %convert_bitcast_fusion.weights_ref, bf16[16,32,16,128]{3,2,1,0:T(8,128)(2,1)} %copy-done.2, bf16[16,32,16,128]{3,2,1,0:T(8,128)(2,1)} %copy-done.2, bf16[16,32,48,128]{3,2,1,0:T(8,128)(2,1)} %all-to-all-done.1.refs_2_.refs_3_, ...), custom_call_target="tpu_custom_call" | custom-call | flops 8589934592 | bytes 41943040 | tf_op jit(solution)/shard_map/beamform/pallas_call | solution.py:231
  313.3 339.9 %all-to-all-done.2.refs_0_.refs_1_ = bf16[16,32,64,384]{3,2,1,0:T(8,128)(2,1)} async-done(((bf16[16,32,64,384]{3,2,1,0:T(8,128)(2,1)}), bf16[16,32,64,384]{3,2,1,0:T(8,128)(2,1)}, u32[]{:S(2)}, u32[]{:S(2)}) %all-to-all-start.2) | async-done | bytes 25165856 | tf_op jit(solution)/shard_map/all_to_all | solution.py:365
  653.2 104.0 %all-to-all-start.3 = ((bf16[16,16,2,32,128]{4,3,2,1,0:T(8,128)(2,1)}), bf16[16,16,2,32,128]{4,3,2,1,0:T(8,128)(2,1)}, u32[]{:S(2)}, u32[]{:S(2)}) async-start(bf16[16,16,2,32,128]{4,3,2,1,0:T(8,128)(2,1)} %beamform.5), calls=%async_computation.3 | async-start | bytes 8388608 | tf_op jit(solution)/shard_map/all_to_all | solution.py:365
  757.2 42.8 %beamform.4 = bf16[16,16,2,32,256]{4,3,2,1,0:T(8,128)(2,1)} custom-call(bf16[16,2,512,1024]{3,2,1,0:T(8,128)(2,1)} %convert_bitcast_fusion.weights_ref, bf16[16,32,64,384]{3,2,1,0:T(8,128)(2,1)} %all-to-all-done.2.refs_0_.refs_1_, bf16[16,32,64,384]{3,2,1,0:T(8,128)(2,1)} %all-to-all-done.2.refs_0_.refs_1_), custom_call_target="tpu_custom_call" | custom-call | flops 17179869184 | bytes 50331648 | tf_op jit(solution)/shard_map/beamform/pallas_call | solution.py:231
  800.0 34.9 %all-to-all-done.3.refs_2_ = bf16[16,16,2,32,128]{4,3,2,1,0:T(8,128)(2,1)} async-done(((bf16[16,16,2,32,128]{4,3,2,1,0:T(8,128)(2,1)}), bf16[16,16,2,32,128]{4,3,2,1,0:T(8,128)(2,1)}, u32[]{:S(2)}, u32[]{:S(2)}) %all-to-all-start.3) | async-done | bytes 4194336 | tf_op jit(solution)/shard_map/all_to_all | solution.py:365
  834.9 19.7 %all-to-all-start.4 = ((bf16[16,16,2,32,256]{4,3,2,1,0:T(8,128)(2,1)}), bf16[16,16,2,32,256]{4,3,2,1,0:T(8,128)(2,1)}, u32[]{:S(2)}, u32[]{:S(2)}) async-start(bf16[16,16,2,32,256]{4,3,2,1,0:T(8,128)(2,1)} %beamform.4), calls=%async_computation.4 | async-start | bytes 16777216 | tf_op jit(solution)/shard_map/all_to_all | solution.py:365
  860.0 17.4 %beamform.7 = bf16[16,12,2,32,128]{4,3,2,1,0:T(8,128)(2,1)} custom-call(bf16[16,2,512,1024]{3,2,1,0:T(8,128)(2,1)} %convert_bitcast_fusion.weights_ref, bf16[16,32,64,384]{3,2,1,0:T(8,128)(2,1)} %all-to-all-done.2.refs_0_.refs_1_, bf16[16,32,64,384]{3,2,1,0:T(8,128)(2,1)} %all-to-all-done.2.refs_0_.refs_1_), custom_call_target="tpu_custom_call" | custom-call | flops 6442450944 | bytes 31457280 | tf_op jit(solution)/shard_map/beamform/pallas_call | solution.py:231
  877.4 71.2 %collective-permute-done.1.refs_0_ = bf16[16,16,2,32,128]{4,3,2,1,0:T(8,128)(2,1)} collective-permute-done((bf16[16,16,2,32,128]{4,3,2,1,0:T(8,128)(2,1)}, bf16[16,16,2,32,128]{4,3,2,1,0:T(8,128)(2,1)}, u32[]{:S(2)}, u32[]{:S(2)}) %collective-permute-start.1) | collective-permute-done | bytes 4194336 | tf_op jit(solution)/shard_map/ppermute | solution.py:21
  948.7 56.7 %all-to-all-done.4.refs_1_.refs_2_.refs_0_ = bf16[16,16,2,32,256]{4,3,2,1,0:T(8,128)(2,1)} async-done(((bf16[16,16,2,32,256]{4,3,2,1,0:T(8,128)(2,1)}), bf16[16,16,2,32,256]{4,3,2,1,0:T(8,128)(2,1)}, u32[]{:S(2)}, u32[]{:S(2)}) %all-to-all-start.4) | async-done | bytes 8388640 | tf_op jit(solution)/shard_map/all_to_all | solution.py:365
  1005.3 36.5 %all-to-all-start.5 = ((bf16[16,12,2,32,128]{4,3,2,1,0:T(8,128)(2,1)}), bf16[16,12,2,32,128]{4,3,2,1,0:T(8,128)(2,1)S(1)}, u32[]{:S(2)}, u32[]{:S(2)}) async-start(bf16[16,12,2,32,128]{4,3,2,1,0:T(8,128)(2,1)} %beamform.7), calls=%async_computation.5 | async-start | bytes 6291456 | tf_op jit(solution)/shard_map/all_to_all | solution.py:365
  1052.2 23.3 %dedisperse.3.refs_9_ = f32[16,16,2,32,512]{4,3,2,1,0:T(8,128)} custom-call(bf16[16,16,2,32,128]{4,3,2,1,0:T(8,128)(2,1)} %collective-permute-done.1.refs_0_, bf16[16,16,2,32,256]{4,3,2,1,0:T(8,128)(2,1)} %all-to-all-done.4.refs_1_.refs_2_.refs_0_, bf16[16,16,2,32,256]{4,3,2,1,0:T(8,128)(2,1)} %all-to-all-done.4.refs_1_.refs_2_.refs_0_, ...), custom_call_target="tpu_custom_call" | custom-call | flops 12884901888 | bytes 46137344 | tf_op jit(solution)/shard_map/dedisperse/pallas_call | solution.py:303
  1075.5 25.7 %all-to-all-done.5.refs_1_ = bf16[16,12,2,32,128]{4,3,2,1,0:T(8,128)(2,1)S(1)} async-done(((bf16[16,12,2,32,128]{4,3,2,1,0:T(8,128)(2,1)}), bf16[16,12,2,32,128]{4,3,2,1,0:T(8,128)(2,1)S(1)}, u32[]{:S(2)}, u32[]{:S(2)}) %all-to-all-start.5) | async-done | bytes 3145760 | tf_op jit(solution)/shard_map/all_to_all | solution.py:365
  1101.2 15.5 %all-to-all-start.6 = ((bf16[16,4,2,32,128]{4,3,2,1,0:T(8,128)(2,1)}), bf16[16,4,2,32,128]{4,3,2,1,0:T(8,128)(2,1)}, u32[]{:S(2)}, u32[]{:S(2)}) async-start(bf16[16,4,2,32,128]{4,3,2,1,0:T(8,128)(2,1)} %beamform.6), calls=%async_computation.6 | async-start | bytes 2097152 | tf_op jit(solution)/shard_map/all_to_all | solution.py:365
  1116.7 18.2 %dedisperse.4.refs_9_ = f32[16,16,2,32,512]{4,3,2,1,0:T(8,128)} custom-call(bf16[16,16,2,32,256]{4,3,2,1,0:T(8,128)(2,1)} %all-to-all-done.4.refs_1_.refs_2_.refs_0_, bf16[16,12,2,32,128]{4,3,2,1,0:T(8,128)(2,1)} %copy-done.3, bf16[16,16,2,32,128]{4,3,2,1,0:T(8,128)(2,1)} %all-to-all-done.3.refs_2_, ...), custom_call_target="tpu_custom_call", output_to_operand_aliasing={{}: (9, {})} | custom-call | flops 9663676416 | bytes 34603008 | tf_op jit(solution)/shard_map/dedisperse/pallas_call | solution.py:303
  (33 shorter events, 45.9 us)
Async XLA Ops:
  0.0 210.4 %copy-start = (s32[1024]{0:T(1024)S(1)}, s32[1024]{0:T(1024)}, u32[]{:S(2)}) copy-start(s32[1024]{0:T(1024)} %param.11) | copy-start | bytes 12292
  8.2 48.5 %all-to-all-start = ((bf16[16,32,16,128]{3,2,1,0:T(8,128)(2,1)}), bf16[16,32,16,128]{3,2,1,0:T(8,128)(2,1)S(1)}, u32[]{:S(2)}, u32[]{:S(2)}) async-start(bf16[16,32,16,128]{3,2,1,0:T(8,128)(2,1)} %bitcast.18), calls=%async_computation | async-start | bytes 4194304 | tf_op jit(solution)/shard_map/all_to_all | solution.py:365
  56.7 93.1 %copy-start.2 = (bf16[16,32,16,128]{3,2,1,0:T(8,128)(2,1)}, bf16[16,32,16,128]{3,2,1,0:T(8,128)(2,1)S(1)}, u32[]{:S(2)}) copy-start(bf16[16,32,16,128]{3,2,1,0:T(8,128)(2,1)S(1)} %all-to-all-done.refs_0_.refs_1_) | copy-start | bytes 6291460
  56.7 125.5 %all-to-all-start.1 = ((bf16[16,32,48,128]{3,2,1,0:T(8,128)(2,1)}), bf16[16,32,48,128]{3,2,1,0:T(8,128)(2,1)}, u32[]{:S(2)}, u32[]{:S(2)}) async-start(bf16[16,32,48,128]{3,2,1,0:T(8,128)(2,1)} %bitcast.17), calls=%async_computation.1 | async-start | bytes 12582912 | tf_op jit(solution)/shard_map/all_to_all | solution.py:365
  69.0 15.1 %collective-permute-start = (bf16[64,4096]{1,0:T(8,128)(2,1)S(1)}, bf16[64,4096]{1,0:T(8,128)(2,1)S(1)}, u32[]{:S(2)}, u32[]{:S(2)}) collective-permute-start(bf16[64,4096]{1,0:T(8,128)(2,1)S(1)} %slice.13), channel_id=1, source_target_pairs={{0,16},{1,17},{2,18},{3,19},{4,20},{5,21},{6,22},{7,23},{8,24},{9,... | collective-permute-start | bytes 1572872 | tf_op jit(solution)/shard_map/ppermute | solution.py:21
  84.1 0.8 copy-start.5
  182.1 28.3 %copy-start.4 = (s32[1024]{0:T(1024)S(1)}, s32[1024]{0:T(1024)}, u32[]{:S(2)}) copy-start(s32[1024]{0:T(1024)} %constant.52) | copy-start | bytes 12292
  182.1 32.9 %copy-start.6 = (s32[32]{0:T(128)S(1)}, s32[32]{0:T(128)}, u32[]{:S(2)}) copy-start(s32[32]{0:T(128)} %param.12) | copy-start | bytes 388
  182.1 471.1 %all-to-all-start.2 = ((bf16[16,32,64,384]{3,2,1,0:T(8,128)(2,1)}), bf16[16,32,64,384]{3,2,1,0:T(8,128)(2,1)}, u32[]{:S(2)}, u32[]{:S(2)}) async-start(bf16[16,32,64,384]{3,2,1,0:T(8,128)(2,1)} %bitcast.16), calls=%async_computation.2 | async-start | bytes 50331648 | tf_op jit(solution)/shard_map/all_to_all | solution.py:365
  653.2 181.7 %all-to-all-start.3 = ((bf16[16,16,2,32,128]{4,3,2,1,0:T(8,128)(2,1)}), bf16[16,16,2,32,128]{4,3,2,1,0:T(8,128)(2,1)}, u32[]{:S(2)}, u32[]{:S(2)}) async-start(bf16[16,16,2,32,128]{4,3,2,1,0:T(8,128)(2,1)} %beamform.5), calls=%async_computation.3 | async-start | bytes 8388608 | tf_op jit(solution)/shard_map/all_to_all | solution.py:365
  834.9 170.4 %all-to-all-start.4 = ((bf16[16,16,2,32,256]{4,3,2,1,0:T(8,128)(2,1)}), bf16[16,16,2,32,256]{4,3,2,1,0:T(8,128)(2,1)}, u32[]{:S(2)}, u32[]{:S(2)}) async-start(bf16[16,16,2,32,256]{4,3,2,1,0:T(8,128)(2,1)} %beamform.4), calls=%async_computation.4 | async-start | bytes 16777216 | tf_op jit(solution)/shard_map/all_to_all | solution.py:365
  854.6 94.0 %collective-permute-start.1 = (bf16[16,16,2,32,128]{4,3,2,1,0:T(8,128)(2,1)}, bf16[16,16,2,32,128]{4,3,2,1,0:T(8,128)(2,1)}, u32[]{:S(2)}, u32[]{:S(2)}) collective-permute-start(bf16[16,16,2,32,128]{4,3,2,1,0:T(8,128)(2,1)} %all-to-all-done.3.refs_2_), channel_id=1, source_target_pairs={{0,16},{1,17},{2,18},{3,19},{4,20},{5,21},{6,22},{7,23},{8,24},{9,... | collective-permute-start | bytes 12582920 | tf_op jit(solution)/shard_map/ppermute | solution.py:21
  1005.3 95.9 %all-to-all-start.5 = ((bf16[16,12,2,32,128]{4,3,2,1,0:T(8,128)(2,1)}), bf16[16,12,2,32,128]{4,3,2,1,0:T(8,128)(2,1)S(1)}, u32[]{:S(2)}, u32[]{:S(2)}) async-start(bf16[16,12,2,32,128]{4,3,2,1,0:T(8,128)(2,1)} %beamform.7), calls=%async_computation.5 | async-start | bytes 6291456 | tf_op jit(solution)/shard_map/all_to_all | solution.py:365
  1101.2 15.5 %copy-start.3 = (bf16[16,12,2,32,128]{4,3,2,1,0:T(8,128)(2,1)}, bf16[16,12,2,32,128]{4,3,2,1,0:T(8,128)(2,1)S(1)}, u32[]{:S(2)}) copy-start(bf16[16,12,2,32,128]{4,3,2,1,0:T(8,128)(2,1)S(1)} %all-to-all-done.5.refs_1_) | copy-start | bytes 9437188
  1101.2 38.5 %all-to-all-start.6 = ((bf16[16,4,2,32,128]{4,3,2,1,0:T(8,128)(2,1)}), bf16[16,4,2,32,128]{4,3,2,1,0:T(8,128)(2,1)}, u32[]{:S(2)}, u32[]{:S(2)}) async-start(bf16[16,4,2,32,128]{4,3,2,1,0:T(8,128)(2,1)} %beamform.6), calls=%async_computation.6 | async-start | bytes 2097152 | tf_op jit(solution)/shard_map/all_to_all | solution.py:365
  1139.7 8.0 copy-start.1

commit v2 on v1

--- a/solution.py
+++ b/solution.py
@@ -12,6 +12,7 @@
 DFT_LEN = 256
 GAP = 8
 ANTENNA_BLOCK = 16
+MERGED = 512
 VMEM_LIMIT = 56 * 1024 * 1024
 
 
@@ -282,7 +283,7 @@
     count = len(pieces) - 1
     groups, per_target, beams, length = chirp[0].shape
     advance = length // 2
-    sources = max(1, min(groups, 1024 // (beams * chans)))
+    sources = max(1, min(groups, MERGED // (beams * chans)))
 
     def piece_spec(block, start):
         skip = (low - start) // chans
@@ -381,24 +382,19 @@
     value, chirp = lax.optimization_barrier((value, chirp))
     series_last = previous = exchange(value, previous)
     leading = shifted(series_last, "section", 1)
-    value = form([received_rest], cuts, 0, last - 1, advance, *whole)
-    series_early = previous = exchange(value, previous)
-
-    tail = max(1, per_target // 4)
+
+    tail = max(1, per_target // 8)
     middle = per_target - tail
-    value = form([received_rest], cuts, last - 1, 1, advance, 0, middle)
+    value = form([received_rest], cuts, 0, last, advance, 0, middle)
+    series_head = previous = exchange(value, previous)
+    value = form([received_rest], cuts, 0, last, advance, middle, per_target)
     value, leading = lax.optimization_barrier((value, leading))
-    series_head = previous = exchange(value, previous)
-    value = form([received_rest], cuts, last - 1, 1, advance, middle, per_target)
-    early = [(leading, 0, 0)] + [(series_early, m, 0) for m in range(last - 1)]
-    output = dedisperse(early, 0, blocks, 0, per_target, tail, chirp, tables, None)
-    value, output = lax.optimization_barrier((value, output))
     series_tail = exchange(value, previous)
 
-    before, after = (series_early, last - 2, 0), (series_last, 0, 0)
+    output = None
     for low, high, series in ((0, middle, series_head), (middle, per_target, series_tail)):
-        pieces = [before, (series, 0, low), after]
-        output = dedisperse(pieces, last - 1, blocks, low, high, tail, chirp, tables, output)
+        pieces = [(leading, 0, 0)] + [(series, m, low) for m in range(last)] + [(series_last, 0, 0)]
+        output = dedisperse(pieces, 0, blocks, low, high, tail, chirp, tables, output)
     return output.reshape((channels,) + output.shape[2:])
 
 

time: 1150 us -> 1150 us (level)
  waiting for transfers between devices: 600 us -> 619 us
  Pallas kernels: 230 us -> 212 us
    pallas_call x4 -> x3, Pallas kernels: 89.6 us -> 79.2 us  [beamform(): pl.pallas_call(functools.partial(beamform_kernel, cuts), grid=(high - low...]
    all_to_all x7 -> x6, waiting for transfers between devices: 517 us -> 527 us  [exchange(): return lax.all_to_all(value, 'grp', split_axis=0, concat_axis=0, tiled=True)]
    pallas_call x3 -> x2, Pallas kernels: 49.5 us -> 41.5 us  [dedisperse(): pl.pallas_call(functools.partial(dedisperse_kernel, count), grid=(groups...]
    all_to_all x7 -> x6, starting transfers between devices: 223 us -> 218 us  [exchange(): return lax.all_to_all(value, 'grp', split_axis=0, concat_axis=0, tiled=True)]
  transfers between devices with their start and end apart: 9 -> 8, of which waited for: 9 -> 7; matrix products, arithmetic and copies ran while one was open for 7% -> 7% of each run, Pallas kernels for 19% -> 17%
where the time goes in v2:
time: 1150 us; the launch traced here: 1140 us
  waiting for transfers between devices  619 us (54%)
  starting transfers between devices  226 us (20%)
  Pallas kernels  212 us (18%)
  matrix products  43.5 us (4%)
  other arithmetic  35.7 us (3%)
    all_to_all x6, waiting for transfers between devices, exchange(): return lax.all_to_all(value, 'grp', split_axis=0, concat_axis=0, tiled=True)  527 us
    all_to_all x6, starting transfers between devices, exchange(): return lax.all_to_all(value, 'grp', split_axis=0, concat_axis=0, tiled=True)  218 us
    ppermute x2, waiting for transfers between devices, shifted(): lax.ppermute(value, axis, [(source, source + steps) for source in range(l...  92 us
    pallas_call x3, Pallas kernels, channelise(): pl.pallas_call(functools.partial(channelise_kernel, taps, frame, spectra,...  91.3 us
    pallas_call x3, Pallas kernels, beamform(): pl.pallas_call(functools.partial(beamform_kernel, cuts), grid=(high - low...  79.2 us
    dot_general x1, matrix products, local(): jnp.einsum('ckba,ar->ckbr', beam_weights, chosen, preferred_element_type=...  43.5 us
    pallas_call x2, Pallas kernels, dedisperse(): pl.pallas_call(functools.partial(dedisperse_kernel, count), grid=(groups...  41.5 us
    sin x1, other arithmetic, chirp_factor(): return (jnp.cos(phases), jnp.sin(phases))  31.9 us
  transfers between devices with their start and end apart: 8, of which 7 were waited for; matrix products, arithmetic and copies ran while one was open for 7% of the time, Pallas kernels for 17%

profile of v2, /device:TPU:0, one launch (start us, length us, event | category | flops | bytes accessed | tf_op | source)
XLA Modules:
  0.0 1144.6 jit_solution(1175108207699708868)
XLA Ops:
  0.0 8.1 channelise.5
  8.1 7.4 all-to-all-start
  15.5 18.3 %channelise.4 = bf16[512,48,128]{2,1,0:T(8,128)(2,1)} custom-call(f32[8,512]{1,0:T(8,128)} %refs_0_.5, bf16[512,512]{1,0:T(8,128)(2,1)} %constant.48.clone.refs_1_, bf16[64,262144]{1,0:T(8,128)(2,1)} %refs_3_.5, bf16[64,262144]{1,0:T(8,128)(2,1)} %refs_3_.5), custom_call_target="tpu_custom_call" | custom-call | flops 6442450944 | bytes 12582912 | tf_op jit(solution)/shard_map/channelise/pallas_call | solution.py:168
  33.8 22.8 %all-to-all-done.refs_0_.refs_1_ = bf16[16,32,16,128]{3,2,1,0:T(8,128)(2,1)S(1)} async-done(((bf16[16,32,16,128]{3,2,1,0:T(8,128)(2,1)}), bf16[16,32,16,128]{3,2,1,0:T(8,128)(2,1)S(1)}, u32[]{:S(2)}, u32[]{:S(2)}) %all-to-all-start) | async-done | bytes 2097184 | tf_op jit(solution)/shard_map/all_to_all | solution.py:366
  56.6 11.3 all-to-all-start.1
  72.5 11.6 %collective-permute-done.refs_4_ = bf16[64,4096]{1,0:T(8,128)(2,1)S(1)} collective-permute-done((bf16[64,4096]{1,0:T(8,128)(2,1)S(1)}, bf16[64,4096]{1,0:T(8,128)(2,1)S(1)}, u32[]{:S(2)}, u32[]{:S(2)}) %collective-permute-start) | collective-permute-done | bytes 524320 | tf_op jit(solution)/shard_map/ppermute | solution.py:22
  84.9 64.9 %channelise.3 = bf16[512,64,384]{2,1,0:T(8,128)(2,1)} custom-call(f32[8,512]{1,0:T(8,128)} %refs_0_.5, bf16[512,512]{1,0:T(8,128)(2,1)} %constant.48.clone.refs_1_, bf16[64,262144]{1,0:T(8,128)(2,1)} %refs_3_.5, bf16[64,262144]{1,0:T(8,128)(2,1)} %refs_3_.5, bf16[64,4096]{1,0:T(8,128)(2,1)} %copy-done.5), custom_call_target="tpu_custom_call" | custom-call | flops 25769803776 | bytes 50331648 | tf_op jit(solution)/shard_map/channelise/pallas_call | solution.py:168
  149.8 32.3 %all-to-all-done.1.refs_2_.refs_3_ = bf16[16,32,48,128]{3,2,1,0:T(8,128)(2,1)} async-done(((bf16[16,32,48,128]{3,2,1,0:T(8,128)(2,1)}), bf16[16,32,48,128]{3,2,1,0:T(8,128)(2,1)}, u32[]{:S(2)}, u32[]{:S(2)}) %all-to-all-start.1) | async-done | bytes 6291488 | tf_op jit(solution)/shard_map/all_to_all | solution.py:366
  182.1 28.3 %all-to-all-start.2 = ((bf16[16,32,64,384]{3,2,1,0:T(8,128)(2,1)}), bf16[16,32,64,384]{3,2,1,0:T(8,128)(2,1)}, u32[]{:S(2)}, u32[]{:S(2)}) async-start(bf16[16,32,64,384]{3,2,1,0:T(8,128)(2,1)} %bitcast.16), calls=%async_computation.2 | async-start | bytes 50331648 | tf_op jit(solution)/shard_map/all_to_all | solution.py:366
  215.1 31.9 %fusion = (f32[16,16,32,256]{3,2,1,0:T(8,128)}, f32[16,16,32,256]{3,2,1,0:T(8,128)}) fusion(f32[256]{0:T(256)S(1)} %get-tuple-element.34, f32[256]{0:T(256)S(1)} %get-tuple-element.33, f32[16,16,32]{2,1,0:T(8,128)S(1)} %broadcast_multiply_fusion), kind=kLoop, calls=%fused_computation.3 | loop fusion | flops 4194304 | bytes 16812032 | tf_op jit(solution)/shard_map/sin | solution.py:67
  247.0 43.5 %convert_bitcast_fusion.weights_ref = bf16[16,2,512,1024]{3,2,1,0:T(8,128)(2,1)} fusion(bf16[16,2,512,1024]{3,2,1,0:T(8,128)(2,1)} %param.10, s32[1024]{0:T(1024)S(1)} %gather_fusion), kind=kOutput, calls=%fused_computation.1 | convolution fusion | flops 34377564160 | bytes 67112960 | tf_op jit(solution)/shard_map/ckba,ar->ckbr/dot_general | solution.py:354
  290.5 22.7 %beamform.4 = bf16[16,16,2,32,128]{4,3,2,1,0:T(8,128)(2,1)} custom-call(bf16[16,2,512,1024]{3,2,1,0:T(8,128)(2,1)} %convert_bitcast_fusion.weights_ref, bf16[16,32,16,128]{3,2,1,0:T(8,128)(2,1)} %copy-done.3, bf16[16,32,16,128]{3,2,1,0:T(8,128)(2,1)} %copy-done.3, bf16[16,32,48,128]{3,2,1,0:T(8,128)(2,1)} %all-to-all-done.1.refs_2_.refs_3_, ...), custom_call_target="tpu_custom_call" | custom-call | flops 8589934592 | bytes 41943040 | tf_op jit(solution)/shard_map/beamform/pallas_call | solution.py:232
  313.2 339.9 %all-to-all-done.2.refs_0_.refs_1_ = bf16[16,32,64,384]{3,2,1,0:T(8,128)(2,1)} async-done(((bf16[16,32,64,384]{3,2,1,0:T(8,128)(2,1)}), bf16[16,32,64,384]{3,2,1,0:T(8,128)(2,1)}, u32[]{:S(2)}, u32[]{:S(2)}) %all-to-all-start.2) | async-done | bytes 25165856 | tf_op jit(solution)/shard_map/all_to_all | solution.py:366
  653.2 104.0 %all-to-all-start.3 = ((bf16[16,16,2,32,128]{4,3,2,1,0:T(8,128)(2,1)}), bf16[16,16,2,32,128]{4,3,2,1,0:T(8,128)(2,1)}, u32[]{:S(2)}, u32[]{:S(2)}) async-start(bf16[16,16,2,32,128]{4,3,2,1,0:T(8,128)(2,1)} %beamform.4), calls=%async_computation.3 | async-start | bytes 8388608 | tf_op jit(solution)/shard_map/all_to_all | solution.py:366
  757.2 48.1 %beamform.5 = bf16[16,14,2,32,384]{4,3,2,1,0:T(8,128)(2,1)} custom-call(bf16[16,2,512,1024]{3,2,1,0:T(8,128)(2,1)} %convert_bitcast_fusion.weights_ref, bf16[16,32,64,384]{3,2,1,0:T(8,128)(2,1)} %all-to-all-done.2.refs_0_.refs_1_, bf16[16,32,64,384]{3,2,1,0:T(8,128)(2,1)} %all-to-all-done.2.refs_0_.refs_1_), custom_call_target="tpu_custom_call" | custom-call | flops 22548578304 | bytes 51380224 | tf_op jit(solution)/shard_map/beamform/pallas_call | solution.py:232
  805.4 29.5 %all-to-all-done.3.refs_4_ = bf16[16,16,2,32,128]{4,3,2,1,0:T(8,128)(2,1)} async-done(((bf16[16,16,2,32,128]{4,3,2,1,0:T(8,128)(2,1)}), bf16[16,16,2,32,128]{4,3,2,1,0:T(8,128)(2,1)}, u32[]{:S(2)}, u32[]{:S(2)}) %all-to-all-start.3) | async-done | bytes 4194336 | tf_op jit(solution)/shard_map/all_to_all | solution.py:366
  834.9 19.7 %all-to-all-start.4 = ((bf16[16,14,2,32,384]{4,3,2,1,0:T(8,128)(2,1)}), bf16[16,14,2,32,384]{4,3,2,1,0:T(8,128)(2,1)}, u32[]{:S(2)}, u32[]{:S(2)}) async-start(bf16[16,14,2,32,384]{4,3,2,1,0:T(8,128)(2,1)} %beamform.5), calls=%async_computation.4 | async-start | bytes 22020096 | tf_op jit(solution)/shard_map/all_to_all | solution.py:366
  854.6 5.4 collective-permute-start.1
  860.0 8.3 beamform.3
  868.3 80.4 %collective-permute-done.1.refs_0_ = bf16[16,16,2,32,128]{4,3,2,1,0:T(8,128)(2,1)} collective-permute-done((bf16[16,16,2,32,128]{4,3,2,1,0:T(8,128)(2,1)}, bf16[16,16,2,32,128]{4,3,2,1,0:T(8,128)(2,1)}, u32[]{:S(2)}, u32[]{:S(2)}) %collective-permute-start.1) | collective-permute-done | bytes 4194336 | tf_op jit(solution)/shard_map/ppermute | solution.py:22
  948.6 102.3 %all-to-all-done.4.refs_1_.refs_2_.refs_3_ = bf16[16,14,2,32,384]{4,3,2,1,0:T(8,128)(2,1)} async-done(((bf16[16,14,2,32,384]{4,3,2,1,0:T(8,128)(2,1)}), bf16[16,14,2,32,384]{4,3,2,1,0:T(8,128)(2,1)}, u32[]{:S(2)}, u32[]{:S(2)}) %all-to-all-start.4) | async-done | bytes 11010080 | tf_op jit(solution)/shard_map/all_to_all | solution.py:366
  1050.9 47.0 %all-to-all-start.5 = ((bf16[16,2,2,32,384]{4,3,2,1,0:T(8,128)(2,1)}), bf16[16,2,2,32,384]{4,3,2,1,0:T(8,128)(2,1)S(1)}, u32[]{:S(2)}, u32[]{:S(2)}) async-start(bf16[16,2,2,32,384]{4,3,2,1,0:T(8,128)(2,1)} %beamform.3), calls=%async_computation.5 | async-start | bytes 3145728 | tf_op jit(solution)/shard_map/all_to_all | solution.py:366
  1101.7 34.1 %dedisperse.2.refs_11_ = f32[16,16,2,32,512]{4,3,2,1,0:T(8,128)} custom-call(bf16[16,16,2,32,128]{4,3,2,1,0:T(8,128)(2,1)} %collective-permute-done.1.refs_0_, bf16[16,14,2,32,384]{4,3,2,1,0:T(8,128)(2,1)} %all-to-all-done.4.refs_1_.refs_2_.refs_3_, bf16[16,14,2,32,384]{4,3,2,1,0:T(8,128)(2,1)} %all-to-all-done.4.refs_1_.refs_2_.refs_3_, ...), custom_call_target="tpu_custom_call" | custom-call | flops 22548578304 | bytes 62390272 | tf_op jit(solution)/shard_map/dedisperse/pallas_call | solution.py:304
  1137.0 7.3 dedisperse.3
  (29 shorter events, 14.9 us)
Async XLA Ops:
  0.0 210.4 %copy-start = (s32[1024]{0:T(1024)S(1)}, s32[1024]{0:T(1024)}, u32[]{:S(2)}) copy-start(s32[1024]{0:T(1024)} %param.11) | copy-start | bytes 12292
  8.1 48.5 %all-to-all-start = ((bf16[16,32,16,128]{3,2,1,0:T(8,128)(2,1)}), bf16[16,32,16,128]{3,2,1,0:T(8,128)(2,1)S(1)}, u32[]{:S(2)}, u32[]{:S(2)}) async-start(bf16[16,32,16,128]{3,2,1,0:T(8,128)(2,1)} %bitcast.18), calls=%async_computation | async-start | bytes 4194304 | tf_op jit(solution)/shard_map/all_to_all | solution.py:366
  56.6 93.1 %copy-start.3 = (bf16[16,32,16,128]{3,2,1,0:T(8,128)(2,1)}, bf16[16,32,16,128]{3,2,1,0:T(8,128)(2,1)S(1)}, u32[]{:S(2)}) copy-start(bf16[16,32,16,128]{3,2,1,0:T(8,128)(2,1)S(1)} %all-to-all-done.refs_0_.refs_1_) | copy-start | bytes 6291460
  56.6 125.5 %all-to-all-start.1 = ((bf16[16,32,48,128]{3,2,1,0:T(8,128)(2,1)}), bf16[16,32,48,128]{3,2,1,0:T(8,128)(2,1)}, u32[]{:S(2)}, u32[]{:S(2)}) async-start(bf16[16,32,48,128]{3,2,1,0:T(8,128)(2,1)} %bitcast.17), calls=%async_computation.1 | async-start | bytes 12582912 | tf_op jit(solution)/shard_map/all_to_all | solution.py:366
  69.0 15.1 %collective-permute-start = (bf16[64,4096]{1,0:T(8,128)(2,1)S(1)}, bf16[64,4096]{1,0:T(8,128)(2,1)S(1)}, u32[]{:S(2)}, u32[]{:S(2)}) collective-permute-start(bf16[64,4096]{1,0:T(8,128)(2,1)S(1)} %slice.13), channel_id=1, source_target_pairs={{0,16},{1,17},{2,18},{3,19},{4,20},{5,21},{6,22},{7,23},{8,24},{9,... | collective-permute-start | bytes 1572872 | tf_op jit(solution)/shard_map/ppermute | solution.py:22
  84.1 0.8 copy-start.5
  182.1 28.3 %copy-start.4 = (s32[1024]{0:T(1024)S(1)}, s32[1024]{0:T(1024)}, u32[]{:S(2)}) copy-start(s32[1024]{0:T(1024)} %constant.52) | copy-start | bytes 12292
  182.1 32.9 %copy-start.6 = (s32[32]{0:T(128)S(1)}, s32[32]{0:T(128)}, u32[]{:S(2)}) copy-start(s32[32]{0:T(128)} %param.12) | copy-start | bytes 388
  182.1 471.1 %all-to-all-start.2 = ((bf16[16,32,64,384]{3,2,1,0:T(8,128)(2,1)}), bf16[16,32,64,384]{3,2,1,0:T(8,128)(2,1)}, u32[]{:S(2)}, u32[]{:S(2)}) async-start(bf16[16,32,64,384]{3,2,1,0:T(8,128)(2,1)} %bitcast.16), calls=%async_computation.2 | async-start | bytes 50331648 | tf_op jit(solution)/shard_map/all_to_all | solution.py:366
  653.2 181.7 %all-to-all-start.3 = ((bf16[16,16,2,32,128]{4,3,2,1,0:T(8,128)(2,1)}), bf16[16,16,2,32,128]{4,3,2,1,0:T(8,128)(2,1)}, u32[]{:S(2)}, u32[]{:S(2)}) async-start(bf16[16,16,2,32,128]{4,3,2,1,0:T(8,128)(2,1)} %beamform.4), calls=%async_computation.3 | async-start | bytes 8388608 | tf_op jit(solution)/shard_map/all_to_all | solution.py:366
  834.9 216.0 %all-to-all-start.4 = ((bf16[16,14,2,32,384]{4,3,2,1,0:T(8,128)(2,1)}), bf16[16,14,2,32,384]{4,3,2,1,0:T(8,128)(2,1)}, u32[]{:S(2)}, u32[]{:S(2)}) async-start(bf16[16,14,2,32,384]{4,3,2,1,0:T(8,128)(2,1)} %beamform.5), calls=%async_computation.4 | async-start | bytes 22020096 | tf_op jit(solution)/shard_map/all_to_all | solution.py:366
  854.6 94.1 %collective-permute-start.1 = (bf16[16,16,2,32,128]{4,3,2,1,0:T(8,128)(2,1)}, bf16[16,16,2,32,128]{4,3,2,1,0:T(8,128)(2,1)}, u32[]{:S(2)}, u32[]{:S(2)}) collective-permute-start(bf16[16,16,2,32,128]{4,3,2,1,0:T(8,128)(2,1)} %all-to-all-done.3.refs_4_), channel_id=1, source_target_pairs={{0,16},{1,17},{2,18},{3,19},{4,20},{5,21},{6,22},{7,23},{8,24},{9,... | collective-permute-start | bytes 12582920 | tf_op jit(solution)/shard_map/ppermute | solution.py:22
  1050.9 84.9 %all-to-all-start.5 = ((bf16[16,2,2,32,384]{4,3,2,1,0:T(8,128)(2,1)}), bf16[16,2,2,32,384]{4,3,2,1,0:T(8,128)(2,1)S(1)}, u32[]{:S(2)}, u32[]{:S(2)}) async-start(bf16[16,2,2,32,384]{4,3,2,1,0:T(8,128)(2,1)} %beamform.3), calls=%async_computation.5 | async-start | bytes 3145728 | tf_op jit(solution)/shard_map/all_to_all | solution.py:366
  1135.9 1.2 copy-start.2
  1137.0 7.3 copy-start.1

commit v3 on v2

--- a/solution.py
+++ b/solution.py
@@ -12,7 +12,7 @@
 DFT_LEN = 256
 GAP = 8
 ANTENNA_BLOCK = 16
-MERGED = 512
+MERGED = 1024
 VMEM_LIMIT = 56 * 1024 * 1024
 
 
@@ -39,20 +39,17 @@
 
 def block_tables(length):
     half_len = length // 2
-    factor = length ** (-0.5)
-    sample = jnp.arange(length, dtype=jnp.int32)
-    angles = (
-        2.0 * math.pi / length * (sample[:, None] * sample[None, :] % length).astype(jnp.float32)
-    )
-    cosine_table = (jnp.cos(angles) * factor).astype(jnp.bfloat16)
-    sine_table = (jnp.sin(angles) * factor).astype(jnp.bfloat16)
-    forward_real = jnp.concatenate([cosine_table, -sine_table], axis=1)
-    forward_imag = jnp.concatenate([sine_table, cosine_table], axis=1)
+    factor = np.float32(length ** (-0.5))
+    sample = np.arange(length)
+    winding = (sample[:, None] * sample[None, :] % length).astype(np.float32)
+    angles = np.float32(2.0 * math.pi / length) * winding
+    cosine_table = np.cos(angles) * factor
+    sine_table = np.sin(angles) * factor
+    forward = np.block([[cosine_table, -sine_table], [sine_table, cosine_table]])
     back_cos = cosine_table[:, half_len:]
     back_sin = sine_table[:, half_len:]
-    inverse_real = jnp.concatenate([back_cos, back_sin], axis=1)
-    inverse_imag = jnp.concatenate([-back_sin, back_cos], axis=1)
-    return (forward_real, forward_imag, inverse_real, inverse_imag)
+    inverse = np.block([[back_cos, back_sin], [-back_sin, back_cos]])
+    return (jnp.asarray(forward.astype(jnp.bfloat16)), jnp.asarray(inverse.astype(jnp.bfloat16)))
 
 
 def chirp_factor(delays, channel_count, channels, length):
@@ -134,7 +131,7 @@
             x_ref[pl.ds(at, frame), :] = result[:, i * spectra : (i + 1) * spectra]
         return carry
 
-    lax.fori_loop(0, rows // 2, transform, 0, unroll=4)
+    lax.fori_loop(0, rows // 2, transform, 0, unroll=8)
 
     def arrange(step, carry):
         for i in range(8):
@@ -142,7 +139,7 @@
             out_ref[j] = x_ref[pl.ds(j, rows, stride=frame + GAP), :].astype(jnp.bfloat16)
         return carry
 
-    lax.fori_loop(0, frame // 8, arrange, 0)
+    lax.fori_loop(0, frame // 8, arrange, 0, unroll=4)
 
 
 def channelise(voltages, halo, filter_taps, table, first, count, spectra, low, high):
@@ -249,7 +246,7 @@
 
 def dedisperse_kernel(count, *refs):
     pieces = refs[: count + 1]
-    cos_ref, sin_ref, fr_ref, fi_ref, ir_ref, ii_ref = refs[count + 1 : count + 7]
+    cos_ref, sin_ref, forward_ref, inverse_ref = refs[count + 1 : count + 5]
     out_ref = refs[-1]
     sources, chans, _, beams, advance = pieces[0].shape
     length = 2 * advance
@@ -264,16 +261,16 @@
         before, after = pieces[m], pieces[m + 1]
         real = jnp.concatenate([part(before, 0), part(after, 0)], axis=1)
         imag = jnp.concatenate([part(before, 1), part(after, 1)], axis=1)
-        spectrum = jnp.dot(real, fr_ref[...], preferred_element_type=jnp.float32) + jnp.dot(
-            imag, fi_ref[...], preferred_element_type=jnp.float32
+        spectrum = jnp.dot(real, forward_ref[:length], preferred_element_type=jnp.float32) + jnp.dot(
+            imag, forward_ref[length:], preferred_element_type=jnp.float32
         )
         spec_real = spectrum[:, :length]
         spec_imag = spectrum[:, length:]
         filtered_real = (spec_real * chirp_real - spec_imag * chirp_imag).astype(jnp.bfloat16)
         filtered_imag = (spec_real * chirp_imag + spec_imag * chirp_real).astype(jnp.bfloat16)
-        result = jnp.dot(filtered_real, ir_ref[...], preferred_element_type=jnp.float32) + jnp.dot(
-            filtered_imag, ii_ref[...], preferred_element_type=jnp.float32
-        )
+        result = jnp.dot(
+            filtered_real, inverse_ref[:length], preferred_element_type=jnp.float32
+        ) + jnp.dot(filtered_imag, inverse_ref[length:], preferred_element_type=jnp.float32)
         at = slice(m * advance, (m + 1) * advance)
         out_ref[:, :, 0, :, at] = result[:, :advance].reshape(sources, chans, beams, advance)
         out_ref[:, :, 1, :, at] = result[:, advance:].reshape(sources, chans, beams, advance)
@@ -283,7 +280,8 @@
     count = len(pieces) - 1
     groups, per_target, beams, length = chirp[0].shape
     advance = length // 2
-    sources = max(1, min(groups, MERGED // (beams * chans)))
+    merged = MERGED if high - low > chans else MERGED // 2
+    sources = max(1, min(groups, merged // (beams * chans)))
 
     def piece_spec(block, start):
         skip = (low - start) // chans

time: 1150 us -> 1140 us (level)
  transfers between devices with their start and end apart: 8 -> 8, of which waited for: 7 -> 7; matrix products, arithmetic and copies ran while one was open for 7% -> 7% of each run, Pallas kernels for 17% -> 16%
where the time goes in v3:
time: 1140 us
  waiting for transfers between devices  626 us (55%)
  starting transfers between devices  226 us (20%)
  Pallas kernels  202 us (18%)
  matrix products  43.5 us (4%)
  other arithmetic  32 us (3%)
    all_to_all x6, waiting for transfers between devices, exchange(): return lax.all_to_all(value, 'grp', split_axis=0, concat_axis=0, tiled=True)  534 us
    all_to_all x6, starting transfers between devices, exchange(): return lax.all_to_all(value, 'grp', split_axis=0, concat_axis=0, tiled=True)  218 us
    ppermute x2, waiting for transfers between devices, shifted(): lax.ppermute(value, axis, [(source, source + steps) for source in range(l...  92 us
    pallas_call x3, Pallas kernels, channelise(): pl.pallas_call(functools.partial(channelise_kernel, taps, frame, spectra,...  83.4 us
    pallas_call x3, Pallas kernels, beamform(): pl.pallas_call(functools.partial(beamform_kernel, cuts), grid=(high - low...  79.2 us
    dot_general x1, matrix products, local(): jnp.einsum('ckba,ar->ckbr', beam_weights, chosen, preferred_element_type=...  43.5 us
    pallas_call x2, Pallas kernels, dedisperse(): pl.pallas_call(functools.partial(dedisperse_kernel, count), grid=(groups...  39.6 us
    sin x1, other arithmetic, chirp_factor(): return (jnp.cos(phases), jnp.sin(phases))  31.9 us
  transfers between devices with their start and end apart: 8, of which 7 were waited for; matrix products, arithmetic and copies ran while one was open for 7% of the time, Pallas kernels for 16%

profile of v3, /device:TPU:0, one launch (start us, length us, event | category | flops | bytes accessed | tf_op | source)
XLA Modules:
  0.0 1138.4 jit_solution(15717804941329399882)
XLA Ops:
  0.0 7.7 channelise.5
  7.7 7.4 all-to-all-start
  15.1 16.8 %channelise.4 = bf16[512,48,128]{2,1,0:T(8,128)(2,1)} custom-call(f32[8,512]{1,0:T(8,128)} %refs_0_.5, bf16[512,512]{1,0:T(8,128)(2,1)} %constant.33.clone.refs_1_, bf16[64,262144]{1,0:T(8,128)(2,1)} %refs_3_.5, bf16[64,262144]{1,0:T(8,128)(2,1)} %refs_3_.5), custom_call_target="tpu_custom_call" | custom-call | flops 6442450944 | bytes 12582912 | tf_op jit(solution)/shard_map/channelise/pallas_call | solution.py:165
  31.9 24.3 %all-to-all-done.refs_0_.refs_1_ = bf16[16,32,16,128]{3,2,1,0:T(8,128)(2,1)S(1)} async-done(((bf16[16,32,16,128]{3,2,1,0:T(8,128)(2,1)}), bf16[16,32,16,128]{3,2,1,0:T(8,128)(2,1)S(1)}, u32[]{:S(2)}, u32[]{:S(2)}) %all-to-all-start) | async-done | bytes 2097184 | tf_op jit(solution)/shard_map/all_to_all | solution.py:364
  56.2 11.3 all-to-all-start.1
  72.0 11.6 %collective-permute-done.refs_4_ = bf16[64,4096]{1,0:T(8,128)(2,1)S(1)} collective-permute-done((bf16[64,4096]{1,0:T(8,128)(2,1)S(1)}, bf16[64,4096]{1,0:T(8,128)(2,1)S(1)}, u32[]{:S(2)}, u32[]{:S(2)}) %collective-permute-start) | collective-permute-done | bytes 524320 | tf_op jit(solution)/shard_map/ppermute | solution.py:22
  84.4 59.0 %channelise.3 = bf16[512,64,384]{2,1,0:T(8,128)(2,1)} custom-call(f32[8,512]{1,0:T(8,128)} %refs_0_.5, bf16[512,512]{1,0:T(8,128)(2,1)} %constant.33.clone.refs_1_, bf16[64,262144]{1,0:T(8,128)(2,1)} %refs_3_.5, bf16[64,262144]{1,0:T(8,128)(2,1)} %refs_3_.5, bf16[64,4096]{1,0:T(8,128)(2,1)} %copy-done.5), custom_call_target="tpu_custom_call" | custom-call | flops 25769803776 | bytes 50331648 | tf_op jit(solution)/shard_map/channelise/pallas_call | solution.py:165
  143.4 38.3 %all-to-all-done.1.refs_2_.refs_3_ = bf16[16,32,48,128]{3,2,1,0:T(8,128)(2,1)} async-done(((bf16[16,32,48,128]{3,2,1,0:T(8,128)(2,1)}), bf16[16,32,48,128]{3,2,1,0:T(8,128)(2,1)}, u32[]{:S(2)}, u32[]{:S(2)}) %all-to-all-start.1) | async-done | bytes 6291488 | tf_op jit(solution)/shard_map/all_to_all | solution.py:364
  181.7 28.3 %all-to-all-start.2 = ((bf16[16,32,64,384]{3,2,1,0:T(8,128)(2,1)}), bf16[16,32,64,384]{3,2,1,0:T(8,128)(2,1)}, u32[]{:S(2)}, u32[]{:S(2)}) async-start(bf16[16,32,64,384]{3,2,1,0:T(8,128)(2,1)} %bitcast.16), calls=%async_computation.2 | async-start | bytes 50331648 | tf_op jit(solution)/shard_map/all_to_all | solution.py:364
  214.6 31.9 %fusion = (f32[16,16,32,256]{3,2,1,0:T(8,128)}, f32[16,16,32,256]{3,2,1,0:T(8,128)}) fusion(f32[256]{0:T(256)S(1)} %get-tuple-element.28, f32[256]{0:T(256)S(1)} %get-tuple-element.27, f32[16,16,32]{2,1,0:T(8,128)S(1)} %broadcast_multiply_fusion), kind=kLoop, calls=%fused_computation.3 | loop fusion | flops 4194304 | bytes 16812032 | tf_op jit(solution)/shard_map/sin | solution.py:64
  246.5 43.5 %convert_bitcast_fusion.weights_ref = bf16[16,2,512,1024]{3,2,1,0:T(8,128)(2,1)} fusion(bf16[16,2,512,1024]{3,2,1,0:T(8,128)(2,1)} %param.12, s32[1024]{0:T(1024)S(1)} %gather_fusion), kind=kOutput, calls=%fused_computation.1 | convolution fusion | flops 34377564160 | bytes 67112960 | tf_op jit(solution)/shard_map/ckba,ar->ckbr/dot_general | solution.py:352
  290.1 22.7 %beamform.4 = bf16[16,16,2,32,128]{4,3,2,1,0:T(8,128)(2,1)} custom-call(bf16[16,2,512,1024]{3,2,1,0:T(8,128)(2,1)} %convert_bitcast_fusion.weights_ref, bf16[16,32,16,128]{3,2,1,0:T(8,128)(2,1)} %copy-done.3, bf16[16,32,16,128]{3,2,1,0:T(8,128)(2,1)} %copy-done.3, bf16[16,32,48,128]{3,2,1,0:T(8,128)(2,1)} %all-to-all-done.1.refs_2_.refs_3_, ...), custom_call_target="tpu_custom_call" | custom-call | flops 8589934592 | bytes 41943040 | tf_op jit(solution)/shard_map/beamform/pallas_call | solution.py:229
  312.8 339.9 %all-to-all-done.2.refs_0_.refs_1_ = bf16[16,32,64,384]{3,2,1,0:T(8,128)(2,1)} async-done(((bf16[16,32,64,384]{3,2,1,0:T(8,128)(2,1)}), bf16[16,32,64,384]{3,2,1,0:T(8,128)(2,1)}, u32[]{:S(2)}, u32[]{:S(2)}) %all-to-all-start.2) | async-done | bytes 25165856 | tf_op jit(solution)/shard_map/all_to_all | solution.py:364
  652.7 104.0 %all-to-all-start.3 = ((bf16[16,16,2,32,128]{4,3,2,1,0:T(8,128)(2,1)}), bf16[16,16,2,32,128]{4,3,2,1,0:T(8,128)(2,1)}, u32[]{:S(2)}, u32[]{:S(2)}) async-start(bf16[16,16,2,32,128]{4,3,2,1,0:T(8,128)(2,1)} %beamform.4), calls=%async_computation.3 | async-start | bytes 8388608 | tf_op jit(solution)/shard_map/all_to_all | solution.py:364
  756.8 48.2 %beamform.5 = bf16[16,14,2,32,384]{4,3,2,1,0:T(8,128)(2,1)} custom-call(bf16[16,2,512,1024]{3,2,1,0:T(8,128)(2,1)} %convert_bitcast_fusion.weights_ref, bf16[16,32,64,384]{3,2,1,0:T(8,128)(2,1)} %all-to-all-done.2.refs_0_.refs_1_, bf16[16,32,64,384]{3,2,1,0:T(8,128)(2,1)} %all-to-all-done.2.refs_0_.refs_1_), custom_call_target="tpu_custom_call" | custom-call | flops 22548578304 | bytes 51380224 | tf_op jit(solution)/shard_map/beamform/pallas_call | solution.py:229
  804.9 29.5 %all-to-all-done.3.refs_4_ = bf16[16,16,2,32,128]{4,3,2,1,0:T(8,128)(2,1)} async-done(((bf16[16,16,2,32,128]{4,3,2,1,0:T(8,128)(2,1)}), bf16[16,16,2,32,128]{4,3,2,1,0:T(8,128)(2,1)}, u32[]{:S(2)}, u32[]{:S(2)}) %all-to-all-start.3) | async-done | bytes 4194336 | tf_op jit(solution)/shard_map/all_to_all | solution.py:364
  834.4 19.7 %all-to-all-start.4 = ((bf16[16,14,2,32,384]{4,3,2,1,0:T(8,128)(2,1)}), bf16[16,14,2,32,384]{4,3,2,1,0:T(8,128)(2,1)}, u32[]{:S(2)}, u32[]{:S(2)}) async-start(bf16[16,14,2,32,384]{4,3,2,1,0:T(8,128)(2,1)} %beamform.5), calls=%async_computation.4 | async-start | bytes 22020096 | tf_op jit(solution)/shard_map/all_to_all | solution.py:364
  854.1 5.4 collective-permute-start.1
  859.5 8.3 beamform.3
  867.8 80.3 %collective-permute-done.1.refs_0_ = bf16[16,16,2,32,128]{4,3,2,1,0:T(8,128)(2,1)} collective-permute-done((bf16[16,16,2,32,128]{4,3,2,1,0:T(8,128)(2,1)}, bf16[16,16,2,32,128]{4,3,2,1,0:T(8,128)(2,1)}, u32[]{:S(2)}, u32[]{:S(2)}) %collective-permute-start.1) | collective-permute-done | bytes 4194336 | tf_op jit(solution)/shard_map/ppermute | solution.py:22
  948.2 102.3 %all-to-all-done.4.refs_1_.refs_2_.refs_3_ = bf16[16,14,2,32,384]{4,3,2,1,0:T(8,128)(2,1)} async-done(((bf16[16,14,2,32,384]{4,3,2,1,0:T(8,128)(2,1)}), bf16[16,14,2,32,384]{4,3,2,1,0:T(8,128)(2,1)}, u32[]{:S(2)}, u32[]{:S(2)}) %all-to-all-start.4) | async-done | bytes 11010080 | tf_op jit(solution)/shard_map/all_to_all | solution.py:364
  1050.5 47.0 %all-to-all-start.5 = ((bf16[16,2,2,32,384]{4,3,2,1,0:T(8,128)(2,1)}), bf16[16,2,2,32,384]{4,3,2,1,0:T(8,128)(2,1)S(1)}, u32[]{:S(2)}, u32[]{:S(2)}) async-start(bf16[16,2,2,32,384]{4,3,2,1,0:T(8,128)(2,1)} %beamform.3), calls=%async_computation.5 | async-start | bytes 3145728 | tf_op jit(solution)/shard_map/all_to_all | solution.py:364
  1097.5 32.2 %dedisperse.2.refs_9_ = f32[16,16,2,32,512]{4,3,2,1,0:T(8,128)} custom-call(bf16[16,16,2,32,128]{4,3,2,1,0:T(8,128)(2,1)} %collective-permute-done.1.refs_0_, bf16[16,14,2,32,384]{4,3,2,1,0:T(8,128)(2,1)} %all-to-all-done.4.refs_1_.refs_2_.refs_3_, bf16[16,14,2,32,384]{4,3,2,1,0:T(8,128)(2,1)} %all-to-all-done.4.refs_1_.refs_2_.refs_3_, ...), custom_call_target="tpu_custom_call" | custom-call | flops 22548578304 | bytes 62390272 | tf_op jit(solution)/shard_map/dedisperse/pallas_call | solution.py:302
  1130.9 7.3 dedisperse.3
  (23 shorter events, 11.1 us)
Async XLA Ops:
  0.0 209.9 %copy-start = (s32[1024]{0:T(1024)S(1)}, s32[1024]{0:T(1024)}, u32[]{:S(2)}) copy-start(s32[1024]{0:T(1024)} %param.13) | copy-start | bytes 12292
  7.7 48.5 %all-to-all-start = ((bf16[16,32,16,128]{3,2,1,0:T(8,128)(2,1)}), bf16[16,32,16,128]{3,2,1,0:T(8,128)(2,1)S(1)}, u32[]{:S(2)}, u32[]{:S(2)}) async-start(bf16[16,32,16,128]{3,2,1,0:T(8,128)(2,1)} %bitcast.18), calls=%async_computation | async-start | bytes 4194304 | tf_op jit(solution)/shard_map/all_to_all | solution.py:364
  56.2 87.2 %copy-start.3 = (bf16[16,32,16,128]{3,2,1,0:T(8,128)(2,1)}, bf16[16,32,16,128]{3,2,1,0:T(8,128)(2,1)S(1)}, u32[]{:S(2)}) copy-start(bf16[16,32,16,128]{3,2,1,0:T(8,128)(2,1)S(1)} %all-to-all-done.refs_0_.refs_1_) | copy-start | bytes 6291460
  56.2 125.5 %all-to-all-start.1 = ((bf16[16,32,48,128]{3,2,1,0:T(8,128)(2,1)}), bf16[16,32,48,128]{3,2,1,0:T(8,128)(2,1)}, u32[]{:S(2)}, u32[]{:S(2)}) async-start(bf16[16,32,48,128]{3,2,1,0:T(8,128)(2,1)} %bitcast.17), calls=%async_computation.1 | async-start | bytes 12582912 | tf_op jit(solution)/shard_map/all_to_all | solution.py:364
  68.5 15.1 %collective-permute-start = (bf16[64,4096]{1,0:T(8,128)(2,1)S(1)}, bf16[64,4096]{1,0:T(8,128)(2,1)S(1)}, u32[]{:S(2)}, u32[]{:S(2)}) collective-permute-start(bf16[64,4096]{1,0:T(8,128)(2,1)S(1)} %slice.3), channel_id=1, source_target_pairs={{0,16},{1,17},{2,18},{3,19},{4,20},{5,21},{6,22},{7,23},{8,24},{9,... | collective-permute-start | bytes 1572872 | tf_op jit(solution)/shard_map/ppermute | solution.py:22
  83.6 0.8 copy-start.5
  181.7 28.3 %copy-start.4 = (s32[1024]{0:T(1024)S(1)}, s32[1024]{0:T(1024)}, u32[]{:S(2)}) copy-start(s32[1024]{0:T(1024)} %constant.39) | copy-start | bytes 12292
  181.7 32.9 %copy-start.6 = (s32[32]{0:T(128)S(1)}, s32[32]{0:T(128)}, u32[]{:S(2)}) copy-start(s32[32]{0:T(128)} %param.14) | copy-start | bytes 388
  181.7 471.1 %all-to-all-start.2 = ((bf16[16,32,64,384]{3,2,1,0:T(8,128)(2,1)}), bf16[16,32,64,384]{3,2,1,0:T(8,128)(2,1)}, u32[]{:S(2)}, u32[]{:S(2)}) async-start(bf16[16,32,64,384]{3,2,1,0:T(8,128)(2,1)} %bitcast.16), calls=%async_computation.2 | async-start | bytes 50331648 | tf_op jit(solution)/shard_map/all_to_all | solution.py:364
  652.7 181.7 %all-to-all-start.3 = ((bf16[16,16,2,32,128]{4,3,2,1,0:T(8,128)(2,1)}), bf16[16,16,2,32,128]{4,3,2,1,0:T(8,128)(2,1)}, u32[]{:S(2)}, u32[]{:S(2)}) async-start(bf16[16,16,2,32,128]{4,3,2,1,0:T(8,128)(2,1)} %beamform.4), calls=%async_computation.3 | async-start | bytes 8388608 | tf_op jit(solution)/shard_map/all_to_all | solution.py:364
  834.4 216.1 %all-to-all-start.4 = ((bf16[16,14,2,32,384]{4,3,2,1,0:T(8,128)(2,1)}), bf16[16,14,2,32,384]{4,3,2,1,0:T(8,128)(2,1)}, u32[]{:S(2)}, u32[]{:S(2)}) async-start(bf16[16,14,2,32,384]{4,3,2,1,0:T(8,128)(2,1)} %beamform.5), calls=%async_computation.4 | async-start | bytes 22020096 | tf_op jit(solution)/shard_map/all_to_all | solution.py:364
  854.1 94.0 %collective-permute-start.1 = (bf16[16,16,2,32,128]{4,3,2,1,0:T(8,128)(2,1)}, bf16[16,16,2,32,128]{4,3,2,1,0:T(8,128)(2,1)}, u32[]{:S(2)}, u32[]{:S(2)}) collective-permute-start(bf16[16,16,2,32,128]{4,3,2,1,0:T(8,128)(2,1)} %all-to-all-done.3.refs_4_), channel_id=1, source_target_pairs={{0,16},{1,17},{2,18},{3,19},{4,20},{5,21},{6,22},{7,23},{8,24},{9,... | collective-permute-start | bytes 12582920 | tf_op jit(solution)/shard_map/ppermute | solution.py:22
  1050.5 79.3 %all-to-all-start.5 = ((bf16[16,2,2,32,384]{4,3,2,1,0:T(8,128)(2,1)}), bf16[16,2,2,32,384]{4,3,2,1,0:T(8,128)(2,1)S(1)}, u32[]{:S(2)}, u32[]{:S(2)}) async-start(bf16[16,2,2,32,384]{4,3,2,1,0:T(8,128)(2,1)} %beamform.3), calls=%async_computation.5 | async-start | bytes 3145728 | tf_op jit(solution)/shard_map/all_to_all | solution.py:364
  1129.7 1.2 copy-start.2
  1130.9 7.3 copy-start.1

commit v4 on v3

--- a/solution.py
+++ b/solution.py
@@ -14,6 +14,7 @@
 ANTENNA_BLOCK = 16
 MERGED = 1024
 VMEM_LIMIT = 56 * 1024 * 1024
+SMALL_VMEM_LIMIT = 28 * 1024 * 1024
 
 
 def shifted(value, axis, steps):
@@ -280,7 +281,8 @@
     count = len(pieces) - 1
     groups, per_target, beams, length = chirp[0].shape
     advance = length // 2
-    merged = MERGED if high - low > chans else MERGED // 2
+    large = high - low > chans
+    merged = MERGED if large else MERGED // 2
     sources = max(1, min(groups, merged // (beams * chans)))
 
     def piece_spec(block, start):
@@ -311,7 +313,9 @@
             (groups, per_target, 2, beams, blocks * advance), jnp.float32
         ),
         input_output_aliases=aliases,
-        compiler_params=pltpu.CompilerParams(vmem_limit_bytes=VMEM_LIMIT),
+        compiler_params=pltpu.CompilerParams(
+            vmem_limit_bytes=VMEM_LIMIT if large else SMALL_VMEM_LIMIT
+        ),
         cost_estimate=pl.CostEstimate(
             flops=12 * count * groups * (high - low) * beams * length * length,
             bytes_accessed=groups * (high - low) * beams * advance * (12 * count + 20),

time: 1140 us -> 1140 us (level)
  no operation moved by 1% of the time
where the time goes in v4:
time: 1140 us
  waiting for transfers between devices  626 us (55%)
  starting transfers between devices  226 us (20%)
  Pallas kernels  202 us (18%)
  matrix products  43.5 us (4%)
  other arithmetic  32 us (3%)
    all_to_all x6, waiting for transfers between devices, exchange(): return lax.all_to_all(value, 'grp', split_axis=0, concat_axis=0, tiled=True)  534 us
    all_to_all x6, starting transfers between devices, exchange(): return lax.all_to_all(value, 'grp', split_axis=0, concat_axis=0, tiled=True)  218 us
    ppermute x2, waiting for transfers between devices, shifted(): lax.ppermute(value, axis, [(source, source + steps) for source in range(l...  92 us
    pallas_call x3, Pallas kernels, channelise(): pl.pallas_call(functools.partial(channelise_kernel, taps, frame, spectra,...  83.4 us
    pallas_call x3, Pallas kernels, beamform(): pl.pallas_call(functools.partial(beamform_kernel, cuts), grid=(high - low...  79.2 us
    dot_general x1, matrix products, local(): jnp.einsum('ckba,ar->ckbr', beam_weights, chosen, preferred_element_type=...  43.5 us
    pallas_call x2, Pallas kernels, dedisperse(): pl.pallas_call(functools.partial(dedisperse_kernel, count), grid=(groups...  39.1 us
    sin x1, other arithmetic, chirp_factor(): return (jnp.cos(phases), jnp.sin(phases))  31.9 us
  transfers between devices with their start and end apart: 8, of which 7 were waited for; matrix products, arithmetic and copies ran while one was open for 7% of the time, Pallas kernels for 16%

profile of v4, /device:TPU:0, one launch (start us, length us, event | category | flops | bytes accessed | tf_op | source)
XLA Modules:
  0.0 1140.1 jit_solution(1742303560481532111)
XLA Ops:
  0.0 7.7 channelise.5
  7.7 7.4 all-to-all-start
  15.1 16.8 %channelise.4 = bf16[512,48,128]{2,1,0:T(8,128)(2,1)} custom-call(f32[8,512]{1,0:T(8,128)} %refs_0_.5, bf16[512,512]{1,0:T(8,128)(2,1)} %constant.33.clone.refs_1_, bf16[64,262144]{1,0:T(8,128)(2,1)} %refs_3_.5, bf16[64,262144]{1,0:T(8,128)(2,1)} %refs_3_.5), custom_call_target="tpu_custom_call" | custom-call | flops 6442450944 | bytes 12582912 | tf_op jit(solution)/shard_map/channelise/pallas_call | solution.py:166
  31.9 24.3 %all-to-all-done.refs_0_.refs_1_ = bf16[16,32,16,128]{3,2,1,0:T(8,128)(2,1)S(1)} async-done(((bf16[16,32,16,128]{3,2,1,0:T(8,128)(2,1)}), bf16[16,32,16,128]{3,2,1,0:T(8,128)(2,1)S(1)}, u32[]{:S(2)}, u32[]{:S(2)}) %all-to-all-start) | async-done | bytes 2097184 | tf_op jit(solution)/shard_map/all_to_all | solution.py:368
  56.2 11.3 all-to-all-start.1
  72.0 11.6 %collective-permute-done.refs_4_ = bf16[64,4096]{1,0:T(8,128)(2,1)S(1)} collective-permute-done((bf16[64,4096]{1,0:T(8,128)(2,1)S(1)}, bf16[64,4096]{1,0:T(8,128)(2,1)S(1)}, u32[]{:S(2)}, u32[]{:S(2)}) %collective-permute-start) | collective-permute-done | bytes 524320 | tf_op jit(solution)/shard_map/ppermute | solution.py:23
  84.4 59.0 %channelise.3 = bf16[512,64,384]{2,1,0:T(8,128)(2,1)} custom-call(f32[8,512]{1,0:T(8,128)} %refs_0_.5, bf16[512,512]{1,0:T(8,128)(2,1)} %constant.33.clone.refs_1_, bf16[64,262144]{1,0:T(8,128)(2,1)} %refs_3_.5, bf16[64,262144]{1,0:T(8,128)(2,1)} %refs_3_.5, bf16[64,4096]{1,0:T(8,128)(2,1)} %copy-done.7), custom_call_target="tpu_custom_call" | custom-call | flops 25769803776 | bytes 50331648 | tf_op jit(solution)/shard_map/channelise/pallas_call | solution.py:166
  143.4 38.3 %all-to-all-done.1.refs_2_.refs_3_ = bf16[16,32,48,128]{3,2,1,0:T(8,128)(2,1)} async-done(((bf16[16,32,48,128]{3,2,1,0:T(8,128)(2,1)}), bf16[16,32,48,128]{3,2,1,0:T(8,128)(2,1)}, u32[]{:S(2)}, u32[]{:S(2)}) %all-to-all-start.1) | async-done | bytes 6291488 | tf_op jit(solution)/shard_map/all_to_all | solution.py:368
  181.7 28.3 %all-to-all-start.2 = ((bf16[16,32,64,384]{3,2,1,0:T(8,128)(2,1)}), bf16[16,32,64,384]{3,2,1,0:T(8,128)(2,1)}, u32[]{:S(2)}, u32[]{:S(2)}) async-start(bf16[16,32,64,384]{3,2,1,0:T(8,128)(2,1)} %bitcast.16), calls=%async_computation.2 | async-start | bytes 50331648 | tf_op jit(solution)/shard_map/all_to_all | solution.py:368
  214.7 31.9 %fusion = (f32[16,16,32,256]{3,2,1,0:T(8,128)}, f32[16,16,32,256]{3,2,1,0:T(8,128)}) fusion(f32[256]{0:T(256)S(1)} %get-tuple-element.28, f32[256]{0:T(256)S(1)} %get-tuple-element.27, f32[16,16,32]{2,1,0:T(8,128)S(1)} %broadcast_multiply_fusion), kind=kLoop, calls=%fused_computation.3 | loop fusion | flops 4194304 | bytes 16812032 | tf_op jit(solution)/shard_map/sin | solution.py:65
  246.5 43.5 %convert_bitcast_fusion.weights_ref = bf16[16,2,512,1024]{3,2,1,0:T(8,128)(2,1)} fusion(bf16[16,2,512,1024]{3,2,1,0:T(8,128)(2,1)} %param.12, s32[1024]{0:T(1024)S(1)} %gather_fusion), kind=kOutput, calls=%fused_computation.1 | convolution fusion | flops 34377564160 | bytes 67112960 | tf_op jit(solution)/shard_map/ckba,ar->ckbr/dot_general | solution.py:356
  290.1 22.7 %beamform.4 = bf16[16,16,2,32,128]{4,3,2,1,0:T(8,128)(2,1)} custom-call(bf16[16,2,512,1024]{3,2,1,0:T(8,128)(2,1)} %convert_bitcast_fusion.weights_ref, bf16[16,32,16,128]{3,2,1,0:T(8,128)(2,1)} %copy-done.5, bf16[16,32,16,128]{3,2,1,0:T(8,128)(2,1)} %copy-done.5, bf16[16,32,48,128]{3,2,1,0:T(8,128)(2,1)} %all-to-all-done.1.refs_2_.refs_3_, ...), custom_call_target="tpu_custom_call" | custom-call | flops 8589934592 | bytes 41943040 | tf_op jit(solution)/shard_map/beamform/pallas_call | solution.py:230
  312.8 340.0 %all-to-all-done.2.refs_0_.refs_1_ = bf16[16,32,64,384]{3,2,1,0:T(8,128)(2,1)} async-done(((bf16[16,32,64,384]{3,2,1,0:T(8,128)(2,1)}), bf16[16,32,64,384]{3,2,1,0:T(8,128)(2,1)}, u32[]{:S(2)}, u32[]{:S(2)}) %all-to-all-start.2) | async-done | bytes 25165856 | tf_op jit(solution)/shard_map/all_to_all | solution.py:368
  652.8 104.0 %all-to-all-start.3 = ((bf16[16,16,2,32,128]{4,3,2,1,0:T(8,128)(2,1)}), bf16[16,16,2,32,128]{4,3,2,1,0:T(8,128)(2,1)}, u32[]{:S(2)}, u32[]{:S(2)}) async-start(bf16[16,16,2,32,128]{4,3,2,1,0:T(8,128)(2,1)} %beamform.4), calls=%async_computation.3 | async-start | bytes 8388608 | tf_op jit(solution)/shard_map/all_to_all | solution.py:368
  756.8 48.2 %beamform.5 = bf16[16,14,2,32,384]{4,3,2,1,0:T(8,128)(2,1)} custom-call(bf16[16,2,512,1024]{3,2,1,0:T(8,128)(2,1)} %convert_bitcast_fusion.weights_ref, bf16[16,32,64,384]{3,2,1,0:T(8,128)(2,1)} %all-to-all-done.2.refs_0_.refs_1_, bf16[16,32,64,384]{3,2,1,0:T(8,128)(2,1)} %all-to-all-done.2.refs_0_.refs_1_), custom_call_target="tpu_custom_call" | custom-call | flops 22548578304 | bytes 51380224 | tf_op jit(solution)/shard_map/beamform/pallas_call | solution.py:230
  804.9 29.5 %all-to-all-done.3.refs_4_ = bf16[16,16,2,32,128]{4,3,2,1,0:T(8,128)(2,1)} async-done(((bf16[16,16,2,32,128]{4,3,2,1,0:T(8,128)(2,1)}), bf16[16,16,2,32,128]{4,3,2,1,0:T(8,128)(2,1)}, u32[]{:S(2)}, u32[]{:S(2)}) %all-to-all-start.3) | async-done | bytes 4194336 | tf_op jit(solution)/shard_map/all_to_all | solution.py:368
  834.5 19.7 %all-to-all-start.4 = ((bf16[16,14,2,32,384]{4,3,2,1,0:T(8,128)(2,1)}), bf16[16,14,2,32,384]{4,3,2,1,0:T(8,128)(2,1)}, u32[]{:S(2)}, u32[]{:S(2)}) async-start(bf16[16,14,2,32,384]{4,3,2,1,0:T(8,128)(2,1)} %beamform.5), calls=%async_computation.4 | async-start | bytes 22020096 | tf_op jit(solution)/shard_map/all_to_all | solution.py:368
  854.2 5.4 collective-permute-start.1
  859.5 8.3 beamform.3
  867.8 80.4 %collective-permute-done.1.refs_0_ = bf16[16,16,2,32,128]{4,3,2,1,0:T(8,128)(2,1)} collective-permute-done((bf16[16,16,2,32,128]{4,3,2,1,0:T(8,128)(2,1)}, bf16[16,16,2,32,128]{4,3,2,1,0:T(8,128)(2,1)}, u32[]{:S(2)}, u32[]{:S(2)}) %collective-permute-start.1) | collective-permute-done | bytes 4194336 | tf_op jit(solution)/shard_map/ppermute | solution.py:23
  948.2 102.3 %all-to-all-done.4.refs_1_.refs_2_.refs_3_ = bf16[16,14,2,32,384]{4,3,2,1,0:T(8,128)(2,1)} async-done(((bf16[16,14,2,32,384]{4,3,2,1,0:T(8,128)(2,1)}), bf16[16,14,2,32,384]{4,3,2,1,0:T(8,128)(2,1)}, u32[]{:S(2)}, u32[]{:S(2)}) %all-to-all-start.4) | async-done | bytes 11010080 | tf_op jit(solution)/shard_map/all_to_all | solution.py:368
  1050.5 47.0 %all-to-all-start.5 = ((bf16[16,2,2,32,384]{4,3,2,1,0:T(8,128)(2,1)}), bf16[16,2,2,32,384]{4,3,2,1,0:T(8,128)(2,1)S(1)}, u32[]{:S(2)}, u32[]{:S(2)}) async-start(bf16[16,2,2,32,384]{4,3,2,1,0:T(8,128)(2,1)} %beamform.3), calls=%async_computation.5 | async-start | bytes 3145728 | tf_op jit(solution)/shard_map/all_to_all | solution.py:368
  1097.6 32.3 %dedisperse.2.refs_9_ = f32[16,16,2,32,512]{4,3,2,1,0:T(8,128)} custom-call(bf16[16,16,2,32,128]{4,3,2,1,0:T(8,128)(2,1)} %collective-permute-done.1.refs_0_, bf16[16,14,2,32,384]{4,3,2,1,0:T(8,128)(2,1)} %all-to-all-done.4.refs_1_.refs_2_.refs_3_, bf16[16,14,2,32,384]{4,3,2,1,0:T(8,128)(2,1)} %all-to-all-done.4.refs_1_.refs_2_.refs_3_, ...), custom_call_target="tpu_custom_call" | custom-call | flops 22548578304 | bytes 62390272 | tf_op jit(solution)/shard_map/dedisperse/pallas_call | solution.py:304
  1133.3 6.9 dedisperse.3
  (27 shorter events, 13.4 us)
Async XLA Ops:
  0.0 210.0 %copy-start = (s32[1024]{0:T(1024)S(1)}, s32[1024]{0:T(1024)}, u32[]{:S(2)}) copy-start(s32[1024]{0:T(1024)} %param.13) | copy-start | bytes 12292
  7.7 48.5 %all-to-all-start = ((bf16[16,32,16,128]{3,2,1,0:T(8,128)(2,1)}), bf16[16,32,16,128]{3,2,1,0:T(8,128)(2,1)S(1)}, u32[]{:S(2)}, u32[]{:S(2)}) async-start(bf16[16,32,16,128]{3,2,1,0:T(8,128)(2,1)} %bitcast.18), calls=%async_computation | async-start | bytes 4194304 | tf_op jit(solution)/shard_map/all_to_all | solution.py:368
  56.2 87.2 %copy-start.5 = (bf16[16,32,16,128]{3,2,1,0:T(8,128)(2,1)}, bf16[16,32,16,128]{3,2,1,0:T(8,128)(2,1)S(1)}, u32[]{:S(2)}) copy-start(bf16[16,32,16,128]{3,2,1,0:T(8,128)(2,1)S(1)} %all-to-all-done.refs_0_.refs_1_) | copy-start | bytes 6291460
  56.2 125.5 %all-to-all-start.1 = ((bf16[16,32,48,128]{3,2,1,0:T(8,128)(2,1)}), bf16[16,32,48,128]{3,2,1,0:T(8,128)(2,1)}, u32[]{:S(2)}, u32[]{:S(2)}) async-start(bf16[16,32,48,128]{3,2,1,0:T(8,128)(2,1)} %bitcast.17), calls=%async_computation.1 | async-start | bytes 12582912 | tf_op jit(solution)/shard_map/all_to_all | solution.py:368
  68.6 15.1 %collective-permute-start = (bf16[64,4096]{1,0:T(8,128)(2,1)S(1)}, bf16[64,4096]{1,0:T(8,128)(2,1)S(1)}, u32[]{:S(2)}, u32[]{:S(2)}) collective-permute-start(bf16[64,4096]{1,0:T(8,128)(2,1)S(1)} %slice.3), channel_id=1, source_target_pairs={{0,16},{1,17},{2,18},{3,19},{4,20},{5,21},{6,22},{7,23},{8,24},{9,... | collective-permute-start | bytes 1572872 | tf_op jit(solution)/shard_map/ppermute | solution.py:23
  83.6 0.8 copy-start.7
  181.7 28.3 %copy-start.6 = (s32[1024]{0:T(1024)S(1)}, s32[1024]{0:T(1024)}, u32[]{:S(2)}) copy-start(s32[1024]{0:T(1024)} %constant.39) | copy-start | bytes 12292
  181.7 32.9 %copy-start.8 = (s32[32]{0:T(128)S(1)}, s32[32]{0:T(128)}, u32[]{:S(2)}) copy-start(s32[32]{0:T(128)} %param.14) | copy-start | bytes 388
  181.7 471.1 %all-to-all-start.2 = ((bf16[16,32,64,384]{3,2,1,0:T(8,128)(2,1)}), bf16[16,32,64,384]{3,2,1,0:T(8,128)(2,1)}, u32[]{:S(2)}, u32[]{:S(2)}) async-start(bf16[16,32,64,384]{3,2,1,0:T(8,128)(2,1)} %bitcast.16), calls=%async_computation.2 | async-start | bytes 50331648 | tf_op jit(solution)/shard_map/all_to_all | solution.py:368
  652.8 181.7 %all-to-all-start.3 = ((bf16[16,16,2,32,128]{4,3,2,1,0:T(8,128)(2,1)}), bf16[16,16,2,32,128]{4,3,2,1,0:T(8,128)(2,1)}, u32[]{:S(2)}, u32[]{:S(2)}) async-start(bf16[16,16,2,32,128]{4,3,2,1,0:T(8,128)(2,1)} %beamform.4), calls=%async_computation.3 | async-start | bytes 8388608 | tf_op jit(solution)/shard_map/all_to_all | solution.py:368
  834.5 216.0 %all-to-all-start.4 = ((bf16[16,14,2,32,384]{4,3,2,1,0:T(8,128)(2,1)}), bf16[16,14,2,32,384]{4,3,2,1,0:T(8,128)(2,1)}, u32[]{:S(2)}, u32[]{:S(2)}) async-start(bf16[16,14,2,32,384]{4,3,2,1,0:T(8,128)(2,1)} %beamform.5), calls=%async_computation.4 | async-start | bytes 22020096 | tf_op jit(solution)/shard_map/all_to_all | solution.py:368
  854.2 94.0 %collective-permute-start.1 = (bf16[16,16,2,32,128]{4,3,2,1,0:T(8,128)(2,1)}, bf16[16,16,2,32,128]{4,3,2,1,0:T(8,128)(2,1)}, u32[]{:S(2)}, u32[]{:S(2)}) collective-permute-start(bf16[16,16,2,32,128]{4,3,2,1,0:T(8,128)(2,1)} %all-to-all-done.3.refs_4_), channel_id=1, source_target_pairs={{0,16},{1,17},{2,18},{3,19},{4,20},{5,21},{6,22},{7,23},{8,24},{9,... | collective-permute-start | bytes 12582920 | tf_op jit(solution)/shard_map/ppermute | solution.py:23
  1050.5 79.3 %all-to-all-start.5 = ((bf16[16,2,2,32,384]{4,3,2,1,0:T(8,128)(2,1)}), bf16[16,2,2,32,384]{4,3,2,1,0:T(8,128)(2,1)S(1)}, u32[]{:S(2)}, u32[]{:S(2)}) async-start(bf16[16,2,2,32,384]{4,3,2,1,0:T(8,128)(2,1)} %beamform.3), calls=%async_computation.5 | async-start | bytes 3145728 | tf_op jit(solution)/shard_map/all_to_all | solution.py:368
  1097.5 32.3 %copy-start.3 = (bf16[512,512]{1,0:T(8,128)(2,1)S(1)}, bf16[512,512]{1,0:T(8,128)(2,1)}, u32[]{:S(2)}) copy-start(bf16[512,512]{1,0:T(8,128)(2,1)} %constant.36.clone.refs_7_) | copy-start | bytes 1572868
  1097.6 32.3 %copy-start.4 = (bf16[512,256]{1,0:T(8,128)(2,1)S(1)}, bf16[512,256]{1,0:T(8,128)(2,1)}, u32[]{:S(2)}) copy-start(bf16[512,256]{1,0:T(8,128)(2,1)} %constant.37.clone.refs_8_) | copy-start | bytes 786436
  1129.9 3.4 copy-start.2
  1133.3 6.9 copy-start.1
